TPU v7x, 512 devices: a whole 4x4x16 slice. The times are simulated.
512 devices in a mesh: row: 8 (over x, y_lo), col: 16 (over z), dp: 4 (over y_hi, core).
Axes of the slice: x: 4, y: 4 (y_hi: 2, y_lo: 2; y = y_hi * 2 + y_lo), z: 16, core: 2. Of those that a mesh axis runs over, the one named last changes fastest.
Arguments:
- tokens: bfloat16 [512, 16384], P('dp', 'col'), may hold values from -6 to 6
- block_values: bfloat16 [8, 16, 32, 128, 128], P('row', 'col'), may hold values from -0.21875 to 0.21875
- block_index: int32 [8, 16, 2, 32], P('row', 'col'), may hold values from 0 to 31, as said below
- block_count: int32 [8, 16], P('row', 'col'), may hold values from 4 to 32, as said below
- grad_hidden: bfloat16 [512, 32768], P('dp', ('row', 'col')), may hold values from -3 to 3
Outputs:
- hidden: bfloat16 [512, 32768], P('dp', ('row', 'col'))
- grad_tokens: bfloat16 [512, 16384], P('dp', ('col', 'row'))
- grad_blocks: bfloat16 [8, 16, 32, 128, 128], P('row', 'col', 'dp')
Inputs may be any that keep to these rules, and one draw needn't show every extreme that they name: block_index[r, c, 0, s] is a block row below 32 and block_index[r, c, 1, s] a block column below 8 inside cell (r, c); the live slots of a cell name distinct positions; slots at or past block_count[r, c] are unused. `block_count`: some cell holds exactly 32 live slots in every draw.
All inputs are finite; a program needn't handle non-finite values.
Results may differ from a plain program's by a relative error of at most 0.017.
Values may be sent and summed in bfloat16 or wider, within the bound.
No kernel may reach another device: no remote copies, remote signals or barrier semaphores. Data moves between devices by JAX's collectives and lax.ppermute only.
A program may use at most 64 MiB of HBM per device.

v0:
```python
import jax
import jax.numpy as jnp
from jax import lax
from jax.sharding import PartitionSpec as P

grad_scale = 0.0625


def masked_total(make_terms, segment_ids, live_slots, segments):
    capacity = segment_ids.shape[0]
    slot_terms = jnp.where(live_slots[:, None, None], make_terms(0, capacity), 0.0)
    return jax.ops.segment_sum(slot_terms, segment_ids, num_segments=segments)


def local(tokens, block_values, block_index, block_count, grad_hidden):
    weight_blocks = block_values[0, 0]
    block_rows = block_index[0, 0, 0]
    block_cols = block_index[0, 0, 1]
    live_count = block_count[0, 0]
    capacity = weight_blocks.shape[0]
    block_size = weight_blocks.shape[1]
    token_count = tokens.shape[0]
    col_blocks = tokens.shape[1] // block_size
    piece_blocks = grad_hidden.shape[1] // block_size
    col_devices = lax.axis_size("col")
    dp_devices = lax.axis_size("dp")
    row_blocks = piece_blocks * col_devices
    live_slots = jnp.arange(capacity) < live_count
    token_blocks = tokens.reshape(token_count, col_blocks, block_size)

    def forward_terms(first_slot, number):
        chosen = jnp.take(token_blocks, block_cols, axis=1)
        return jnp.einsum("tsm,snm->stn", chosen, weight_blocks, preferred_element_type=jnp.float32)

    hidden_blocks = masked_total(forward_terms, block_rows, live_slots, row_blocks)
    hidden_part = hidden_blocks.transpose(1, 0, 2).reshape(token_count, row_blocks * block_size)
    hidden = lax.psum_scatter(
        hidden_part.astype(jnp.bfloat16), "col", scatter_dimension=1, tiled=True
    )
    dp_index = lax.axis_index("dp")
    owned_slots = capacity // dp_devices
    own_first = dp_index * owned_slots
    own_live = lax.dynamic_slice_in_dim(live_slots, own_first, owned_slots)
    local_rows = lax.all_gather(grad_hidden, "col", axis=1, tiled=True).reshape(
        token_count, row_blocks, block_size
    )

    def grad_terms(first_slot, number):
        picked = jnp.take(local_rows, block_rows, axis=1)
        return jnp.einsum("tsn,snm->stm", picked, weight_blocks, preferred_element_type=jnp.float32)

    grad_pick = jnp.take(local_rows, block_rows, axis=1)
    token_pick = jnp.take(token_blocks, block_cols, axis=1)
    slot_partial = jnp.einsum(
        "tsn,tsm->snm", grad_pick, token_pick, preferred_element_type=jnp.float32
    )
    weight_sums = lax.psum_scatter(
        slot_partial.astype(jnp.bfloat16), "dp", scatter_dimension=0, tiled=True
    ).astype(jnp.float32)
    feature_blocks = masked_total(grad_terms, block_cols, live_slots, col_blocks)
    feature_part = feature_blocks.transpose(1, 0, 2).reshape(token_count, col_blocks * block_size)
    grad_tokens = lax.psum_scatter(
        feature_part.astype(jnp.bfloat16), "row", scatter_dimension=1, tiled=True
    )
    grad_blocks = jnp.where(own_live[:, None, None], weight_sums * grad_scale, 0.0).astype(
        jnp.bfloat16
    )
    return (hidden, grad_tokens, grad_blocks[None, None])


def solution(mesh):
    in_specs = (
        P("dp", "col"),
        P("row", "col", None, None, None),
        P("row", "col", None, None),
        P("row", "col"),
        P("dp", ("row", "col")),
    )
    out_specs = (
        P("dp", ("row", "col")),
        P("dp", ("col", "row")),
        P("row", "col", "dp", None, None),
    )
    return jax.shard_map(local, mesh=mesh, in_specs=in_specs, out_specs=out_specs, check_vma=False)
```

profile of v0, /device:TPU:24, one launch (start us, length us, event | category | flops | bytes accessed | tf_op | source)
XLA Modules:
  0.0 257.9 jit_solution(12291143587485037593)
XLA Ops:
  7.2 0.0 all-gather.2.cloned.1.call-start
  7.2 1.6 copy.17
  8.9 0.0 all-gather.2.cloned.1.call-update
  8.9 0.0 reduce-scatter.4.cloned.1.call-start
  9.6 1.1 copy.14
  10.7 0.2 copy.15
  10.9 0.8 compare_and_fusion
  11.7 0.7 gather_fusion
  12.5 2.2 convolution_select_fusion.1
  14.7 0.2 broadcast_in_dim.54
  15.0 4.7 %scatter_fusion = f32[32,128,128]{2,1,0:T(8,128)S(1)} fusion(f32[32,128,128]{2,1,0:T(8,128)S(1)} %broadcast_in_dim.54, s32[32]{0:T(128)S(1)} %get-tuple-element.18, f32[32,128,128]{2,1,0:T(8,128)} %convolution_select_fusion.1), kind=kCustom, calls=%fused_computation.2 | custom fusion | flops 524288 | bytes 6291584 | tf_op jit(solution)/shard_map/scatter-add | solution.py:12
  19.7 1.1 convert_bitcast_fusion
  20.8 2.3 copy.16
  23.1 0.0 reduce-scatter.4.cloned.1.call-update
  23.1 0.0 reduce-scatter.6.cloned.1.call-start
  23.1 62.8 %all-gather.2.cloned.1.call-done = bf16[128,4096]{0,1:T(8,128)(2,1)} async-done(((bf16[128,256]{0,1:T(8,128)(2,1)}), bf16[128,4096]{0,1:T(8,128)(2,1)}) %all-gather.2.cloned.1.call-update) | async-done | bytes 1048592 | tf_op jit(solution)/shard_map/all_gather | solution.py:44
  85.9 1.6 copy.18
  87.6 0.7 gather_fusion.1
  88.3 1.8 convolution_select_fusion
  90.2 4.7 %scatter_fusion.1 = f32[8,128,128]{2,1,0:T(8,128)S(1)} fusion(f32[8,128,128]{2,1,0:T(8,128)S(1)} %broadcast_in_dim.56, s32[32]{0:T(128)S(1)} %get-tuple-element.17, f32[32,128,128]{2,1,0:T(8,128)} %convolution_select_fusion), kind=kCustom, calls=%fused_computation.3 | custom fusion | flops 524288 | bytes 6291584 | tf_op jit(solution)/shard_map/scatter-add | solution.py:12
  94.9 0.9 copy.19
  95.8 0.0 reduce-scatter.6.cloned.1.call-update
  95.8 0.0 reduce-scatter.8.cloned.1.call-start
  95.9 2.8 %convolution_convert_fusion = bf16[32,128,128]{2,1,0:T(8,128)(2,1)} fusion(bf16[32,128,128]{2,1,0:T(8,128)(2,1)S(1)} %copy-done.2, pred[32]{0:T(512)(128)(4,1)S(1)} %get-tuple-element.15, bf16[32,128,128]{2,1,0:T(8,128)(2,1)} %copy-done.3, pred[32]{0:T(512)(128)(4,1)S(1)} %get-tuple-element.11), kind=kOutput, calls=%fused_computation.6 | convolution fusion | flops 135790592 | bytes 3145792 | tf_op jit(solution)/shard_map/tsn,tsm->snm/dot_general | solution.py:54
  98.7 0.0 reduce-scatter.8.cloned.1.call-update
  98.7 0.1 dynamic_slice.3
  98.8 57.3 %reduce-scatter.4.cloned.1.call-done = bf16[128,256]{0,1:T(8,128)(2,1)} async-done(((bf16[128,4096]{0,1:T(8,128)(2,1)}), bf16[128,256]{0,1:T(8,128)(2,1)}) %reduce-scatter.4.cloned.1.call-update) | async-done | bytes 65552 | tf_op jit(solution)/shard_map/reduce_scatter | solution.py:37
  156.1 1.6 copy.21
  157.6 42.1 %reduce-scatter.6.cloned.1.call-done = bf16[128,128]{0,1:T(8,128)(2,1)} async-done(((bf16[128,1024]{0,1:T(8,128)(2,1)}), bf16[128,128]{0,1:T(8,128)(2,1)}) %reduce-scatter.6.cloned.1.call-update) | async-done | bytes 32784 | tf_op jit(solution)/shard_map/reduce_scatter | solution.py:62
  199.7 1.5 copy.22
  201.2 48.4 %reduce-scatter.8.cloned.1.call-done = bf16[8,128,128]{2,1,0:T(8,128)(2,1)} async-done(((bf16[32,128,128]{2,1,0:T(8,128)(2,1)}), bf16[8,128,128]{2,1,0:T(8,128)(2,1)}) %reduce-scatter.8.cloned.1.call-update) | async-done | bytes 262160 | tf_op jit(solution)/shard_map/reduce_scatter | solution.py:57
  249.6 1.8 fusion.6
  (15 shorter events, 0.1 us)
Async XLA Ops:
  7.2 5.3 %copy-start = (bf16[1,1,32,128,128]{4,3,2,1,0:T(8,128)(2,1)S(1)}, bf16[1,1,32,128,128]{4,3,2,1,0:T(8,128)(2,1)}, u32[]{:S(2)}) copy-start(bf16[1,1,32,128,128]{4,3,2,1,0:T(8,128)(2,1)} %param.10) | copy-start | bytes 3145732
  7.2 5.3 %copy-start.4 = (s32[1,1,2,32]{3,2,1,0:T(2,128)S(1)}, s32[1,1,2,32]{3,2,1,0:T(2,128)}, u32[]{:S(2)}) copy-start(s32[1,1,2,32]{3,2,1,0:T(2,128)} %param.11) | copy-start | bytes 772
  7.2 78.7 %all-gather.2.cloned.1.call-start = ((), (), s32[]{:S(2)}) async-start(), calls=%async_computation.4 | async-start | bytes 1114112 | tf_op jit(solution)/shard_map/all_gather | solution.py:44
  8.9 147.1 %reduce-scatter.4.cloned.1.call-start = ((), (), s32[]{:S(2)}) async-start(), calls=%async_computation.3 | async-start | bytes 1114112 | tf_op jit(solution)/shard_map/reduce_scatter | solution.py:37
  12.5 2.3 copy-start.1
  23.1 176.6 %reduce-scatter.6.cloned.1.call-start = ((), (), s32[]{:S(2)}) async-start(), calls=%async_computation.5 | async-start | bytes 294912 | tf_op jit(solution)/shard_map/reduce_scatter | solution.py:62
  88.3 1.9 copy-start.3
  90.2 5.7 %copy-start.2 = (bf16[32,128,128]{2,1,0:T(8,128)(2,1)S(1)}, bf16[32,128,128]{2,1,0:T(8,128)(2,1)}, u32[]{:S(2)}) copy-start(bf16[32,128,128]{2,1,0:T(8,128)(2,1)} %copy-done.1) | copy-start | bytes 3145732
  95.8 153.8 %reduce-scatter.8.cloned.1.call-start = ((), (), s32[]{:S(2)}) async-start(), calls=%async_computation.6 | async-start | bytes 1310720 | tf_op jit(solution)/shard_map/reduce_scatter | solution.py:57
Sparse Core Ops, SparseCore 0:
  10.7 75.2 all-gather.1
  88.7 67.2 reduce-scatter.3
  159.7 40.0 reduce-scatter.5
  202.6 46.9 reduce-scatter.7
where the time goes:
time: 261 us; the launch traced here: 258 us
  waiting for transfers between devices  211 us (81%)
  between operations  14.6 us (6%)
  other arithmetic  13.1 us (5%)
  local copies, waits for them, and re-layouts  12.6 us (5%)
  matrix products  6.87 us (3%)
    all_gather x1, waiting for transfers between devices, local(): lax.all_gather(grad_hidden, 'col', axis=1, tiled=True)  62.8 us
    reduce_scatter x1, waiting for transfers between devices, local(): lax.psum_scatter(hidden_part.astype(jnp.bfloat16), 'col', scatter_dimensi...  57.3 us
    reduce_scatter x1, waiting for transfers between devices, local(): lax.psum_scatter(slot_partial.astype(jnp.bfloat16), 'dp', scatter_dimensi...  48.4 us
    reduce_scatter x1, waiting for transfers between devices, local(): lax.psum_scatter(feature_part.astype(jnp.bfloat16), 'row', scatter_dimens...  42.1 us
    scatter-add x2, other arithmetic, masked_total(): return jax.ops.segment_sum(slot_terms, segment_ids, num_segments=segments)  9.33 us
    unnamed x14, local copies, waits for them, and re-layouts  5.84 us
  transfers between devices with their start and end apart: 4, of which 4 were waited for; matrix products, arithmetic and copies ran while one was open for 11% of the time, Pallas kernels for 0%

commit v1 on v0

v1 whole, which is shorter than its diff:
```python
import jax
import jax.numpy as jnp
from jax import lax
from jax.experimental import pallas as pl
from jax.experimental.pallas import tpu as pltpu
from jax.sharding import PartitionSpec as P

grad_scale = 0.0625
block = 128
f32 = jnp.float32
bf16 = jnp.bfloat16


def hidden_kernel(
    index, live_count, plane, core_id, tokens, weights, own, up, down, far, token_blocks, total
):
    capacity = weights.shape[0]
    rows = total.shape[0] - 1
    for m in range(token_blocks.shape[0]):
        token_blocks[m] = tokens[:, m * block : (m + 1) * block]
    for b in range(rows):
        total[b] = jnp.zeros_like(total[b])
    count = live_count[0, 0]
    place = plane[0, 0]
    for s in range(capacity):
        live = s < count
        row = jnp.where(live, index[0, s], rows)
        col = jnp.where(live, index[1, s], 0)
        total[row] += lax.dot_general(
            token_blocks[col], weights[s], (((1,), (1,)), ((), ())), preferred_element_type=f32
        )
    for shift, out in ((1, up), (3, down), (2, far), (0, own)):
        near = lax.rem(place + shift, 4)
        for j in range(out.shape[0]):
            for half in range(2):
                out[j, :, half * block : (half + 1) * block] = total[
                    (j * 4 + near) * 2 + half
                ].astype(bf16)


def grads_kernel(
    index, live_count, plane, core_id, tokens, weights, own, above, below, far,
    features, keep, send, token_blocks, grads, total,
):
    capacity = weights.shape[0]
    cols = total.shape[0] - 1
    count = live_count[0, 0]
    place = plane[0, 0]
    core = core_id[0, 0]
    for m in range(cols):
        token_blocks[m] = tokens[:, m * block : (m + 1) * block]
        total[m] = jnp.zeros_like(total[m])
    for shift, part in ((0, own), (1, above), (3, below), (2, far)):
        near = lax.rem(place + shift, 4)
        for j in range(part.shape[0]):
            for half in range(2):
                grads[(j * 4 + near) * 2 + half] = part[j, :, half * block : (half + 1) * block]
    for n in range(capacity):
        group, other, spot = n % 16 // 8, n // 16, n % 8
        s = group * 16 + jnp.where(other == 0, 1 - core, core) * 8 + spot
        live = s < count
        row = jnp.where(live, index[0, s], 0)
        col = jnp.where(live, index[1, s], 0)
        picked = grads[row]
        product = lax.dot_general(
            picked, token_blocks[col], (((0,), (0,)), ((), ())), preferred_element_type=f32
        )
        out = send if other == 0 else keep
        out[group, spot] = jnp.where(live, product * grad_scale, 0.0).astype(bf16)
        total[jnp.where(live, col, cols)] += jnp.dot(
            picked, weights[s], preferred_element_type=f32
        )
    for m in range(cols):
        features[m] = total[m].astype(bf16)


def call(kernel, outs, scratch, flops, *operands):
    return pl.pallas_call(
        kernel,
        out_shape=[jax.ShapeDtypeStruct(s, bf16) for s in outs],
        in_specs=[pl.BlockSpec(memory_space=pltpu.SMEM)] * 4
        + [pl.BlockSpec(memory_space=pltpu.VMEM)] * (len(operands) - 4),
        out_specs=[pl.BlockSpec(memory_space=pltpu.VMEM)] * len(outs),
        scratch_shapes=[pltpu.VMEM(s, t) for s, t in scratch],
        compiler_params=pltpu.CompilerParams(vmem_limit_bytes=32 * 2**20),
        cost_estimate=pl.CostEstimate(flops=flops, bytes_accessed=2**22, transcendentals=0),
    )(*operands)


def shifted(x, axis, by):
    n = lax.axis_size(axis)
    return lax.ppermute(x, axis, [(i, (i + by) % n) for i in range(n)])


def both_ways(x, by):
    n, parts = lax.axis_size("col"), lax.axis_size("dp")
    pairs = []
    for i in range(n):
        for d in range(parts):
            to = (i + (by if d % 2 == 0 else -by)) % n
            pairs.append((i * parts + d, to * parts + d))
    return lax.ppermute(x, ("col", "dp"), pairs)


def swapped(x, axis, bit):
    return lax.ppermute(x, axis, [(i, i ^ bit) for i in range(lax.axis_size(axis))])


def summed(*parts):
    total = parts[0].astype(f32)
    for part in parts[1:]:
        total = total + part.astype(f32)
    return total.astype(bf16)


def local(tokens, block_values, block_index, block_count, grad_hidden):
    weights = block_values[0, 0]
    capacity = weights.shape[0]
    token_count = tokens.shape[0]
    col_blocks = tokens.shape[1] // block
    planes = lax.axis_size("col")
    rows = planes * (grad_hidden.shape[1] // block)
    place = lax.axis_index("col")
    dp = lax.axis_index("dp")
    core, side = lax.rem(dp, 2), lax.div(dp, 2)
    strided = [[i + 4 * j for j in range(planes // 4)] for i in range(4)]
    quarter = (planes // 4, token_count, grad_hidden.shape[1])
    info = (block_index[0, 0], block_count, place.reshape(1, 1), core.reshape(1, 1))
    blocks = (token_count, block)

    grads_own = lax.all_to_all(
        jnp.broadcast_to(grad_hidden[None], quarter), "col", 0, 0, tiled=True,
        axis_index_groups=strided,
    )
    own, up, down, far = call(
        hidden_kernel,
        [quarter] * 4,
        [((col_blocks, *blocks), bf16), ((rows + 1, *blocks), f32)],
        2 * capacity * token_count * block * block,
        *info, tokens, weights,
    )
    from_below = shifted(up, "col", 1)
    from_above = shifted(down, "col", -1)
    from_far = both_ways(far, 2)
    hidden_near = summed(own, from_below, from_above, from_far)
    grads_own, hidden_near = lax.optimization_barrier((grads_own, hidden_near))
    hidden_parts = lax.all_to_all(hidden_near, "col", 0, 0, tiled=True, axis_index_groups=strided)
    above = shifted(grads_own, "col", -1)
    below = shifted(grads_own, "col", 1)
    across = both_ways(grads_own, 2)

    features, keep, send = call(
        grads_kernel,
        [(col_blocks, *blocks), (2, 8, block, block), (2, 8, block, block)],
        [((col_blocks, *blocks), bf16), ((rows, *blocks), bf16), ((col_blocks + 1, *blocks), f32)],
        4 * capacity * token_count * block * block,
        *info, tokens, weights, grads_own, above, below, across,
    )
    features, send, hidden_parts = lax.optimization_barrier((features, send, hidden_parts))
    chip = summed(keep, swapped(send, "dp", 1))
    feature_parts = lax.all_to_all(features, "row", 0, 0, tiled=True)
    mine = lax.dynamic_index_in_dim(chip, side, 0, keepdims=False)
    theirs = lax.dynamic_index_in_dim(chip, 1 - side, 0, keepdims=False)
    grad_blocks = summed(mine, swapped(theirs, "dp", 2))
    grad_tokens = summed(*[feature_parts[i] for i in range(feature_parts.shape[0])])
    hidden = summed(*[hidden_parts[i] for i in range(planes // 4)])
    return hidden, grad_tokens, grad_blocks[None, None]


def solution(mesh):
    in_specs = (
        P("dp", "col"),
        P("row", "col", None, None, None),
        P("row", "col", None, None),
        P("row", "col"),
        P("dp", ("row", "col")),
    )
    out_specs = (
        P("dp", ("row", "col")),
        P("dp", ("col", "row")),
        P("row", "col", "dp", None, None),
    )
    return jax.shard_map(local, mesh=mesh, in_specs=in_specs, out_specs=out_specs, check_vma=False)
```

time: 261 us -> 105 us (0.40)
  the two profiles are of different devices: /device:TPU:24 before, /device:TPU:1 now
where the time goes in v1:
time: 105 us; the launch traced here: 104 us
  starting transfers between devices  62.5 us (60%)
  waiting for transfers between devices  30.1 us (29%)
  Pallas kernels  3.73 us (4%)
  local copies, waits for them, and re-layouts  3.47 us (3%)
  other arithmetic  3.07 us (3%)
  between operations  1.42 us (1%)
    all_to_all x1, starting transfers between devices, local(): lax.all_to_all(jnp.broadcast_to(grad_hidden[None], quarter), 'col', 0, 0,...  15.8 us
    ppermute x4, starting transfers between devices, shifted(): return lax.ppermute(x, axis, [(i, (i + by) % n) for i in range(n)])  14.5 us
    ppermute x2, waiting for transfers between devices, both_ways(): return lax.ppermute(x, ('col', 'dp'), pairs)  11.8 us
    ppermute x4, waiting for transfers between devices, shifted(): return lax.ppermute(x, axis, [(i, (i + by) % n) for i in range(n)])  11 us
    ppermute x2, starting transfers between devices, both_ways(): return lax.ppermute(x, ('col', 'dp'), pairs)  9.72 us
    ppermute x2, starting transfers between devices, swapped(): lax.ppermute(x, axis, [(i, i ^ bit) for i in range(lax.axis_size(axis))])  9.38 us
    all_to_all x1, starting transfers between devices, local(): lax.all_to_all(hidden_near, 'col', 0, 0, tiled=True, axis_index_groups=st...  8.12 us
    ppermute x2, waiting for transfers between devices, swapped(): lax.ppermute(x, axis, [(i, i ^ bit) for i in range(lax.axis_size(axis))])  5.9 us
  transfers between devices with their start and end apart: 11, of which 6 were waited for; matrix products, arithmetic and copies ran while one was open for 2% of the time, Pallas kernels for 4%

profile of v1, /device:TPU:1, one launch (start us, length us, event | category | flops | bytes accessed | tf_op | source)
XLA Modules:
  0.0 104.3 jit_solution(10368682699606835795)
XLA Ops:
  0.6 1.5 %broadcast_in_dim.4 = bf16[4,128,256]{2,1,0:T(8,128)(2,1)} broadcast(bf16[128,256]{1,0:T(8,128)(2,1)} %param.9), dimensions={1,2} | broadcast | bytes 327680 | tf_op jit(solution)/shard_map/broadcast_in_dim | solution.py:132
  2.2 15.8 %all-to-all-start = ((bf16[4,128,256]{2,1,0:T(8,128)(2,1)}), bf16[4,128,256]{2,1,0:T(8,128)(2,1)S(1)}, u32[]{:S(2)}, u32[]{:S(2)}) async-start(bf16[4,128,256]{2,1,0:T(8,128)(2,1)} %broadcast_in_dim.4), calls=%async_computation | async-start | bytes 524288 | tf_op jit(solution)/shard_map/all_to_all | solution.py:131
  18.6 0.0 copy-start.3
  18.6 0.7 copy-done.3
  19.3 1.2 %copy-done = bf16[1,1,32,128,128]{4,3,2,1,0:T(8,128)(2,1)S(1)} copy-done((bf16[1,1,32,128,128]{4,3,2,1,0:T(8,128)(2,1)S(1)}, bf16[1,1,32,128,128]{4,3,2,1,0:T(8,128)(2,1)}, u32[]{:S(2)}) %copy-start) | copy-done | bytes 1048600
  20.5 1.6 %shard_map.76 = (bf16[4,128,256]{2,1,0:T(8,128)(2,1)S(1)}, bf16[4,128,256]{2,1,0:T(8,128)(2,1)S(1)}, bf16[4,128,256]{2,1,0:T(8,128)(2,1)S(1)}, bf16[4,128,256]{2,1,0:T(8,128)(2,1)S(1)}) custom-call(s32[2,32]{1,0:T(2,128)S(1)} %bitcast.17, s32[1,1]{1,0:T(1,128)S(6)} %copy.8.live_count, s32[1,1]{1,0:T(1,128)} %bitcast.1.plane, s32[1,1]{1,0:T(1,128)} %bitcast.2.core_id, ...), custom_call_target="tpu_custom_call" | custom-call | flops 134217728 | bytes 4194304 | tf_op jit(solution)/shard_map/pallas_call | solution.py:78
  22.1 0.0 copy-start.1
  22.1 2.8 %collective-permute-start = (bf16[4,128,256]{2,1,0:T(8,128)(2,1)S(1)}, bf16[4,128,256]{2,1,0:T(8,128)(2,1)S(1)}, u32[]{:S(2)}, u32[]{:S(2)}) collective-permute-start(bf16[4,128,256]{2,1,0:T(8,128)(2,1)S(1)} %get-tuple-element.16), channel_id=1, source_target_pairs={{0,4},{4,8},{8,12},{12,16},{16,20},{20,24},{24,28},{28,32},{32,36}... | collective-permute-start | bytes 786440 | tf_op jit(solution)/shard_map/ppermute | solution.py:92
  24.9 5.2 %collective-permute-start.1 = (bf16[4,128,256]{2,1,0:T(8,128)(2,1)S(1)}, bf16[4,128,256]{2,1,0:T(8,128)(2,1)S(1)}, u32[]{:S(2)}, u32[]{:S(2)}) collective-permute-start(bf16[4,128,256]{2,1,0:T(8,128)(2,1)S(1)} %get-tuple-element.17), channel_id=1, source_target_pairs={{0,60},{4,0},{8,4},{12,8},{16,12},{20,16},{24,20},{28,24},{32,28},... | collective-permute-start | bytes 786440 | tf_op jit(solution)/shard_map/ppermute | solution.py:92
  30.1 3.8 %collective-permute-start.2 = (bf16[4,128,256]{2,1,0:T(8,128)(2,1)S(1)}, bf16[4,128,256]{2,1,0:T(8,128)(2,1)S(1)}, u32[]{:S(2)}, u32[]{:S(2)}) collective-permute-start(bf16[4,128,256]{2,1,0:T(8,128)(2,1)S(1)} %get-tuple-element.18), channel_id=1, source_target_pairs={{0,8},{1,57},{2,10},{3,59},{4,12},{5,61},{6,14},{7,63},{8,16},{9,1... | collective-permute-start | bytes 786440 | tf_op jit(solution)/shard_map/ppermute | solution.py:102
  33.9 6.0 %collective-permute-done = bf16[4,128,256]{2,1,0:T(8,128)(2,1)S(1)} collective-permute-done((bf16[4,128,256]{2,1,0:T(8,128)(2,1)S(1)}, bf16[4,128,256]{2,1,0:T(8,128)(2,1)S(1)}, u32[]{:S(2)}, u32[]{:S(2)}) %collective-permute-start) | collective-permute-done | bytes 262176 | tf_op jit(solution)/shard_map/ppermute | solution.py:92
  39.9 0.0 collective-permute-done.1
  39.9 5.3 %collective-permute-done.2 = bf16[4,128,256]{2,1,0:T(8,128)(2,1)S(1)} collective-permute-done((bf16[4,128,256]{2,1,0:T(8,128)(2,1)S(1)}, bf16[4,128,256]{2,1,0:T(8,128)(2,1)S(1)}, u32[]{:S(2)}, u32[]{:S(2)}) %collective-permute-start.2) | collective-permute-done | bytes 262176 | tf_op jit(solution)/shard_map/ppermute | solution.py:102
  45.2 0.8 add_convert_fusion.1
  46.1 0.0 all-to-all-done.own
  46.1 8.1 %all-to-all-start.1 = ((bf16[4,128,256]{2,1,0:T(8,128)(2,1)}), bf16[4,128,256]{2,1,0:T(8,128)(2,1)S(1)}, u32[]{:S(2)}, u32[]{:S(2)}) async-start(bf16[4,128,256]{2,1,0:T(8,128)(2,1)} %add_convert_fusion.1), calls=%async_computation.1 | async-start | bytes 524288 | tf_op jit(solution)/shard_map/all_to_all | solution.py:147
  54.2 5.9 %collective-permute-start.5 = (bf16[4,128,256]{2,1,0:T(8,128)(2,1)S(1)}, bf16[4,128,256]{2,1,0:T(8,128)(2,1)S(1)}, u32[]{:S(2)}, u32[]{:S(2)}) collective-permute-start(bf16[4,128,256]{2,1,0:T(8,128)(2,1)S(1)} %all-to-all-done.own), channel_id=1, source_target_pairs={{0,8},{1,57},{2,10},{3,59},{4,12},{5,61},{6,14},{7,63},{8,16},{9,1... | collective-permute-start | bytes 786440 | tf_op jit(solution)/shard_map/ppermute | solution.py:102
  60.1 1.9 %collective-permute-start.4 = (bf16[4,128,256]{2,1,0:T(8,128)(2,1)S(1)}, bf16[4,128,256]{2,1,0:T(8,128)(2,1)S(1)}, u32[]{:S(2)}, u32[]{:S(2)}) collective-permute-start(bf16[4,128,256]{2,1,0:T(8,128)(2,1)S(1)} %all-to-all-done.own), channel_id=1, source_target_pairs={{0,4},{4,8},{8,12},{12,16},{16,20},{20,24},{24,28},{28,32},{32,36}... | collective-permute-start | bytes 786440 | tf_op jit(solution)/shard_map/ppermute | solution.py:92
  62.0 4.6 %collective-permute-start.3 = (bf16[4,128,256]{2,1,0:T(8,128)(2,1)S(1)}, bf16[4,128,256]{2,1,0:T(8,128)(2,1)S(1)}, u32[]{:S(2)}, u32[]{:S(2)}) collective-permute-start(bf16[4,128,256]{2,1,0:T(8,128)(2,1)S(1)} %all-to-all-done.own), channel_id=1, source_target_pairs={{0,60},{4,0},{8,4},{12,8},{16,12},{20,16},{24,20},{28,24},{32,28},... | collective-permute-start | bytes 786440 | tf_op jit(solution)/shard_map/ppermute | solution.py:92
  66.6 6.5 %collective-permute-done.5.far = bf16[4,128,256]{2,1,0:T(8,128)(2,1)S(1)} collective-permute-done((bf16[4,128,256]{2,1,0:T(8,128)(2,1)S(1)}, bf16[4,128,256]{2,1,0:T(8,128)(2,1)S(1)}, u32[]{:S(2)}, u32[]{:S(2)}) %collective-permute-start.5) | collective-permute-done | bytes 262176 | tf_op jit(solution)/shard_map/ppermute | solution.py:102
  73.1 5.1 %collective-permute-done.4.below = bf16[4,128,256]{2,1,0:T(8,128)(2,1)S(1)} collective-permute-done((bf16[4,128,256]{2,1,0:T(8,128)(2,1)S(1)}, bf16[4,128,256]{2,1,0:T(8,128)(2,1)S(1)}, u32[]{:S(2)}, u32[]{:S(2)}) %collective-permute-start.4) | collective-permute-done | bytes 262176 | tf_op jit(solution)/shard_map/ppermute | solution.py:92
  78.2 0.0 collective-permute-done.3.above
  78.2 2.1 %shard_map.77 = (bf16[8,128,128]{2,1,0:T(8,128)(2,1)}, bf16[2,8,128,128]{3,2,1,0:T(8,128)(2,1)S(1)}, bf16[2,8,128,128]{3,2,1,0:T(8,128)(2,1)S(1)}) custom-call(s32[2,32]{1,0:T(2,128)S(1)} %bitcast.18, s32[1,1]{1,0:T(1,128)S(6)} %copy.8.live_count, s32[1,1]{1,0:T(1,128)} %bitcast.1.plane, s32[1,1]{1,0:T(1,128)} %bitcast.2.core_id, ...), custom_call_target="tpu_custom_call" | custom-call | flops 268435456 | bytes 4194304 | tf_op jit(solution)/shard_map/pallas_call | solution.py:78
  80.3 4.8 %collective-permute-start.6 = (bf16[2,8,128,128]{3,2,1,0:T(8,128)(2,1)S(1)}, bf16[2,8,128,128]{3,2,1,0:T(8,128)(2,1)S(1)}, u32[]{:S(2)}, u32[]{:S(2)}) collective-permute-start(bf16[2,8,128,128]{3,2,1,0:T(8,128)(2,1)S(1)} %get-tuple-element.26), channel_id=1, source_target_pairs={{0,1},{1,0},{2,3},{3,2},{4,5},{5,4},{6,7},{7,6},{8,9},{9,8},{10,11... | collective-permute-start | bytes 1572872 | tf_op jit(solution)/shard_map/ppermute | solution.py:106
  85.2 5.0 %all-to-all-start.2 = ((bf16[8,128,128]{2,1,0:T(8,128)(2,1)}), bf16[8,128,128]{2,1,0:T(8,128)(2,1)S(1)}, u32[]{:S(2)}, u32[]{:S(2)}) async-start(bf16[8,128,128]{2,1,0:T(8,128)(2,1)} %get-tuple-element.24), calls=%async_computation.2 | async-start | bytes 524288 | tf_op jit(solution)/shard_map/all_to_all | solution.py:161
  90.2 0.1 add_convert_fusion
  90.4 4.5 %collective-permute-start.7 = (bf16[8,128,128]{2,1,0:T(8,128)(2,1)S(1)}, bf16[8,128,128]{2,1,0:T(8,128)(2,1)S(1)}, u32[]{:S(2)}, u32[]{:S(2)}) collective-permute-start(bf16[8,128,128]{2,1,0:T(8,128)(2,1)S(1)} %dynamic-slice_bitcast_fusion), channel_id=1, source_target_pairs={{0,2},{1,3},{2,0},{3,1},{4,6},{5,7},{6,4},{7,5},{8,10},{9,11},{10,... | collective-permute-start | bytes 786440 | tf_op jit(solution)/shard_map/ppermute | solution.py:106
  95.0 0.7 fusion.2
  95.6 1.3 %all-to-all-done.2 = bf16[8,128,128]{2,1,0:T(8,128)(2,1)S(1)} async-done(((bf16[8,128,128]{2,1,0:T(8,128)(2,1)}), bf16[8,128,128]{2,1,0:T(8,128)(2,1)S(1)}, u32[]{:S(2)}, u32[]{:S(2)}) %all-to-all-start.2) | async-done | bytes 262176 | tf_op jit(solution)/shard_map/all_to_all | solution.py:161
  97.0 0.7 fusion.3
  97.6 5.9 %collective-permute-done.7 = bf16[8,128,128]{2,1,0:T(8,128)(2,1)S(1)} collective-permute-done((bf16[8,128,128]{2,1,0:T(8,128)(2,1)S(1)}, bf16[8,128,128]{2,1,0:T(8,128)(2,1)S(1)}, u32[]{:S(2)}, u32[]{:S(2)}) %collective-permute-start.7) | collective-permute-done | bytes 262176 | tf_op jit(solution)/shard_map/ppermute | solution.py:106
  103.5 0.8 fusion.1
  (7 shorter events, 0.0 us)
Async XLA Ops:
  2.2 16.4 %copy-start.2 = (bf16[128,1024]{1,0:T(8,128)(2,1)S(1)}, bf16[128,1024]{1,0:T(8,128)(2,1)}, u32[]{:S(2)}) copy-start(bf16[128,1024]{1,0:T(8,128)(2,1)} %tokens.3) | copy-start | bytes 786436
  2.2 43.9 %all-to-all-start = ((bf16[4,128,256]{2,1,0:T(8,128)(2,1)}), bf16[4,128,256]{2,1,0:T(8,128)(2,1)S(1)}, u32[]{:S(2)}, u32[]{:S(2)}) async-start(bf16[4,128,256]{2,1,0:T(8,128)(2,1)} %broadcast_in_dim.4), calls=%async_computation | async-start | bytes 524288 | tf_op jit(solution)/shard_map/all_to_all | solution.py:131
  18.6 0.7 copy-start.3
  19.3 1.2 %copy-start = (bf16[1,1,32,128,128]{4,3,2,1,0:T(8,128)(2,1)S(1)}, bf16[1,1,32,128,128]{4,3,2,1,0:T(8,128)(2,1)}, u32[]{:S(2)}) copy-start(bf16[1,1,32,128,128]{4,3,2,1,0:T(8,128)(2,1)} %param.6) | copy-start | bytes 3145732
  22.1 56.1 %copy-start.1 = (bf16[1,1,32,128,128]{4,3,2,1,0:T(8,128)(2,1)S(1)}, bf16[1,1,32,128,128]{4,3,2,1,0:T(8,128)(2,1)}, u32[]{:S(2)}) copy-start(bf16[1,1,32,128,128]{4,3,2,1,0:T(8,128)(2,1)} %param.6) | copy-start | bytes 3145732
  22.1 17.8 %collective-permute-start = (bf16[4,128,256]{2,1,0:T(8,128)(2,1)S(1)}, bf16[4,128,256]{2,1,0:T(8,128)(2,1)S(1)}, u32[]{:S(2)}, u32[]{:S(2)}) collective-permute-start(bf16[4,128,256]{2,1,0:T(8,128)(2,1)S(1)} %get-tuple-element.16), channel_id=1, source_target_pairs={{0,4},{4,8},{8,12},{12,16},{16,20},{20,24},{24,28},{28,32},{32,36}... | collective-permute-start | bytes 786440 | tf_op jit(solution)/shard_map/ppermute | solution.py:92
  24.9 15.0 %collective-permute-start.1 = (bf16[4,128,256]{2,1,0:T(8,128)(2,1)S(1)}, bf16[4,128,256]{2,1,0:T(8,128)(2,1)S(1)}, u32[]{:S(2)}, u32[]{:S(2)}) collective-permute-start(bf16[4,128,256]{2,1,0:T(8,128)(2,1)S(1)} %get-tuple-element.17), channel_id=1, source_target_pairs={{0,60},{4,0},{8,4},{12,8},{16,12},{20,16},{24,20},{28,24},{32,28},... | collective-permute-start | bytes 786440 | tf_op jit(solution)/shard_map/ppermute | solution.py:92
  30.1 15.1 %collective-permute-start.2 = (bf16[4,128,256]{2,1,0:T(8,128)(2,1)S(1)}, bf16[4,128,256]{2,1,0:T(8,128)(2,1)S(1)}, u32[]{:S(2)}, u32[]{:S(2)}) collective-permute-start(bf16[4,128,256]{2,1,0:T(8,128)(2,1)S(1)} %get-tuple-element.18), channel_id=1, source_target_pairs={{0,8},{1,57},{2,10},{3,59},{4,12},{5,61},{6,14},{7,63},{8,16},{9,1... | collective-permute-start | bytes 786440 | tf_op jit(solution)/shard_map/ppermute | solution.py:102
  46.1 34.2 %all-to-all-start.1 = ((bf16[4,128,256]{2,1,0:T(8,128)(2,1)}), bf16[4,128,256]{2,1,0:T(8,128)(2,1)S(1)}, u32[]{:S(2)}, u32[]{:S(2)}) async-start(bf16[4,128,256]{2,1,0:T(8,128)(2,1)} %add_convert_fusion.1), calls=%async_computation.1 | async-start | bytes 524288 | tf_op jit(solution)/shard_map/all_to_all | solution.py:147
  54.2 18.9 %collective-permute-start.5 = (bf16[4,128,256]{2,1,0:T(8,128)(2,1)S(1)}, bf16[4,128,256]{2,1,0:T(8,128)(2,1)S(1)}, u32[]{:S(2)}, u32[]{:S(2)}) collective-permute-start(bf16[4,128,256]{2,1,0:T(8,128)(2,1)S(1)} %all-to-all-done.own), channel_id=1, source_target_pairs={{0,8},{1,57},{2,10},{3,59},{4,12},{5,61},{6,14},{7,63},{8,16},{9,1... | collective-permute-start | bytes 786440 | tf_op jit(solution)/shard_map/ppermute | solution.py:102
  60.1 18.1 %collective-permute-start.4 = (bf16[4,128,256]{2,1,0:T(8,128)(2,1)S(1)}, bf16[4,128,256]{2,1,0:T(8,128)(2,1)S(1)}, u32[]{:S(2)}, u32[]{:S(2)}) collective-permute-start(bf16[4,128,256]{2,1,0:T(8,128)(2,1)S(1)} %all-to-all-done.own), channel_id=1, source_target_pairs={{0,4},{4,8},{8,12},{12,16},{16,20},{20,24},{24,28},{28,32},{32,36}... | collective-permute-start | bytes 786440 | tf_op jit(solution)/shard_map/ppermute | solution.py:92
  62.0 16.1 %collective-permute-start.3 = (bf16[4,128,256]{2,1,0:T(8,128)(2,1)S(1)}, bf16[4,128,256]{2,1,0:T(8,128)(2,1)S(1)}, u32[]{:S(2)}, u32[]{:S(2)}) collective-permute-start(bf16[4,128,256]{2,1,0:T(8,128)(2,1)S(1)} %all-to-all-done.own), channel_id=1, source_target_pairs={{0,60},{4,0},{8,4},{12,8},{16,12},{20,16},{24,20},{28,24},{32,28},... | collective-permute-start | bytes 786440 | tf_op jit(solution)/shard_map/ppermute | solution.py:92
  80.3 9.9 %collective-permute-start.6 = (bf16[2,8,128,128]{3,2,1,0:T(8,128)(2,1)S(1)}, bf16[2,8,128,128]{3,2,1,0:T(8,128)(2,1)S(1)}, u32[]{:S(2)}, u32[]{:S(2)}) collective-permute-start(bf16[2,8,128,128]{3,2,1,0:T(8,128)(2,1)S(1)} %get-tuple-element.26), channel_id=1, source_target_pairs={{0,1},{1,0},{2,3},{3,2},{4,5},{5,4},{6,7},{7,6},{8,9},{9,8},{10,11... | collective-permute-start | bytes 1572872 | tf_op jit(solution)/shard_map/ppermute | solution.py:106
  85.2 11.8 %all-to-all-start.2 = ((bf16[8,128,128]{2,1,0:T(8,128)(2,1)}), bf16[8,128,128]{2,1,0:T(8,128)(2,1)S(1)}, u32[]{:S(2)}, u32[]{:S(2)}) async-start(bf16[8,128,128]{2,1,0:T(8,128)(2,1)} %get-tuple-element.24), calls=%async_computation.2 | async-start | bytes 524288 | tf_op jit(solution)/shard_map/all_to_all | solution.py:161
  90.4 13.1 %collective-permute-start.7 = (bf16[8,128,128]{2,1,0:T(8,128)(2,1)S(1)}, bf16[8,128,128]{2,1,0:T(8,128)(2,1)S(1)}, u32[]{:S(2)}, u32[]{:S(2)}) collective-permute-start(bf16[8,128,128]{2,1,0:T(8,128)(2,1)S(1)} %dynamic-slice_bitcast_fusion), channel_id=1, source_target_pairs={{0,2},{1,3},{2,0},{3,1},{4,6},{5,7},{6,4},{7,5},{8,10},{9,11},{10,... | collective-permute-start | bytes 786440 | tf_op jit(solution)/shard_map/ppermute | solution.py:106

commit v2 on v1

v2 whole, which is shorter than its diff:
```python
import jax
import jax.numpy as jnp
from jax import lax
from jax.experimental import pallas as pl
from jax.experimental.pallas import tpu as pltpu
from jax.sharding import PartitionSpec as P

grad_scale = 0.0625
low_cost = 1000
high_cost = 8 * 10**9
block = 128
f32 = jnp.float32
bf16 = jnp.bfloat16


def hidden_kernel(
    index, live_count, plane, dp_place, tokens, weights, own, up, down, far, token_blocks, total
):
    capacity = weights.shape[0]
    rows = total.shape[0] - 1
    for m in range(token_blocks.shape[0]):
        token_blocks[m] = tokens[:, m * block : (m + 1) * block]
    for b in range(rows):
        total[b] = jnp.zeros_like(total[b])
    count = live_count[0, 0]
    place = plane[0, 0]
    for s in range(capacity):
        live = s < count
        row = jnp.where(live, index[0, s], rows)
        col = jnp.where(live, index[1, s], 0)
        total[row] += lax.dot_general(
            token_blocks[col], weights[s], (((1,), (1,)), ((), ())), preferred_element_type=f32
        )
    far_shift = 2 - 4 * lax.rem(dp_place[0, 0], 2)
    for shift, out in ((1, up), (-1, down), (far_shift, far), (0, own)):
        near = lax.rem(place + shift + 4, 4)
        for a in range(out.shape[0]):
            to = 4 * a + near
            for half in range(2):
                out[a, :, half * block : (half + 1) * block] = total[to * 2 + half].astype(bf16)


def gather_blocks(plane, dp_place, tokens, parts, token_blocks, grads):
    rows = grads.shape[0]
    for m in range(token_blocks.shape[0]):
        token_blocks[m] = tokens[:, m * block : (m + 1) * block]
    far_shift = 4 * lax.rem(dp_place[0, 0], 2) - 2
    for shift, part in zip((0, 1, -1, far_shift), parts):
        near = lax.rem(plane[0, 0] + shift + 4, 4)
        for a in range(part.shape[0]):
            at = 4 * a + near
            for half in range(2):
                grads[at * 2 + half] = part[a, :, half * block : (half + 1) * block]


def blocks_kernel(
    index, live_count, plane, dp_place, tokens, own, above, below, far,
    keep, keep_far, send, token_blocks, grads,
):
    gather_blocks(plane, dp_place, tokens, (own, above, below, far), token_blocks, grads)
    count = live_count[0, 0]
    core = lax.rem(dp_place[0, 0], 2)
    side = lax.div(dp_place[0, 0], 2)
    for n in range(index.shape[1]):
        from_core, from_side, spot = n // 16, n % 16 // 8, n % 8
        owner_core = core if from_core else 1 - core
        owner_side = side if from_side else 1 - side
        s = (owner_side * 2 + owner_core) * 8 + spot
        live = s < count
        product = lax.dot_general(
            grads[jnp.where(live, index[0, s], 0)],
            token_blocks[jnp.where(live, index[1, s], 0)],
            (((0,), (0,)), ((), ())),
            preferred_element_type=f32,
        )
        out = (keep if from_side else keep_far) if from_core else send.at[from_side]
        out[spot] = jnp.where(live, product * grad_scale, 0.0).astype(bf16)


def features_kernel(
    index, live_count, plane, dp_place, tokens, weights, own, above, below, far,
    features, token_blocks, grads, total,
):
    gather_blocks(plane, dp_place, tokens, (own, above, below, far), token_blocks, grads)
    cols = total.shape[0] - 1
    for m in range(cols):
        total[m] = jnp.zeros_like(total[m])
    for s in range(index.shape[1]):
        live = s < live_count[0, 0]
        total[jnp.where(live, index[1, s], cols)] += jnp.dot(
            grads[jnp.where(live, index[0, s], 0)], weights[s], preferred_element_type=f32
        )
    for m in range(cols):
        features[m] = total[m].astype(bf16)


def call(kernel, outs, scratch, flops, *operands):
    return pl.pallas_call(
        kernel,
        out_shape=[jax.ShapeDtypeStruct(s, bf16) for s in outs],
        in_specs=[pl.BlockSpec(memory_space=pltpu.SMEM)] * 4
        + [pl.BlockSpec(memory_space=pltpu.VMEM)] * (len(operands) - 4),
        out_specs=[pl.BlockSpec(memory_space=pltpu.VMEM)] * len(outs),
        scratch_shapes=[pltpu.VMEM(s, t) for s, t in scratch],
        compiler_params=pltpu.CompilerParams(vmem_limit_bytes=32 * 2**20),
        cost_estimate=pl.CostEstimate(flops=flops, bytes_accessed=flops // 256, transcendentals=0),
    )(*operands)


def sum_kernel(parts, out):
    total = parts[0].astype(f32)
    for n in range(1, parts.shape[0]):
        total += parts[n].astype(f32)
    out[...] = total.astype(bf16)


def call_sum(parts, flops):
    return pl.pallas_call(
        sum_kernel,
        out_shape=jax.ShapeDtypeStruct(parts.shape[1:], bf16),
        in_specs=[pl.BlockSpec(memory_space=pltpu.VMEM)],
        out_specs=pl.BlockSpec(memory_space=pltpu.VMEM),
        compiler_params=pltpu.CompilerParams(vmem_limit_bytes=8 * 2**20),
        cost_estimate=pl.CostEstimate(flops=flops, bytes_accessed=flops // 256, transcendentals=0),
    )(parts)


def shifted(x, axis, by):
    n = lax.axis_size(axis)
    return lax.ppermute(x, axis, [(i, (i + by) % n) for i in range(n)])


def both_ways(x, by):
    n, parts = lax.axis_size("col"), lax.axis_size("dp")
    pairs = []
    for i in range(n):
        for d in range(parts):
            to = (i + (by if d % 2 == 0 else -by)) % n
            pairs.append((i * parts + d, to * parts + d))
    return lax.ppermute(x, ("col", "dp"), pairs)


def swapped(x, axis, bit):
    return lax.ppermute(x, axis, [(i, i ^ bit) for i in range(lax.axis_size(axis))])


def summed(*parts):
    total = parts[0].astype(f32)
    for part in parts[1:]:
        total = total + part.astype(f32)
    return total.astype(bf16)


def local(tokens, block_values, block_index, block_count, grad_hidden):
    weights = block_values[0, 0]
    capacity = weights.shape[0]
    token_count = tokens.shape[0]
    col_blocks = tokens.shape[1] // block
    planes = lax.axis_size("col")
    rows = planes * (grad_hidden.shape[1] // block)
    place = lax.axis_index("col")
    dp = lax.axis_index("dp")
    quarter = (planes // 4, token_count, grad_hidden.shape[1])
    info = (block_index[0, 0], block_count, place.reshape(1, 1), dp.reshape(1, 1))
    blocks = (token_count, block)
    owned = (capacity // lax.axis_size("dp"), block, block)

    strided = [[i + 4 * j for j in range(planes // 4)] for i in range(4)]
    copies = jnp.broadcast_to(grad_hidden[None], quarter)
    grads_own = lax.all_to_all(copies, "col", 0, 0, tiled=True, axis_index_groups=strided)
    own, up, down, far = call(
        hidden_kernel,
        [quarter] * 4,
        [((col_blocks, *blocks), bf16), ((rows + 1, *blocks), f32)],
        2 * capacity * token_count * block * block,
        *info, tokens, weights,
    )
    from_below = shifted(up, "col", 1)
    from_above = shifted(down, "col", -1)
    from_far = both_ways(far, 2)
    hidden_near = summed(own, from_below, from_above, from_far)
    grads_own, hidden_near = lax.optimization_barrier((grads_own, hidden_near))
    hidden_parts = lax.all_to_all(hidden_near, "col", 0, 0, tiled=True, axis_index_groups=strided)
    above = shifted(grads_own, "col", -1)
    below = shifted(grads_own, "col", 1)
    across = both_ways(grads_own, 2)
    token_scratch = ((col_blocks, *blocks), bf16)
    grads_scratch = ((rows, *blocks), bf16)
    keep, keep_far, send = call(
        blocks_kernel,
        [owned, owned, (2, *owned)],
        [token_scratch, grads_scratch],
        low_cost,
        *info, tokens, grads_own, above, below, across,
    )
    received = swapped(send, "dp", 1)
    theirs = summed(keep_far, received[0])
    from_side = swapped(theirs, "dp", 2)
    [features] = call(
        features_kernel,
        [(col_blocks, *blocks)],
        [token_scratch, grads_scratch, ((col_blocks + 1, *blocks), f32)],
        low_cost,
        *info, tokens, weights, grads_own, above, below, across,
    )
    hidden = call_sum(hidden_parts, high_cost)
    features, from_side, hidden = lax.optimization_barrier((features, from_side, hidden))
    feature_parts = lax.all_to_all(features, "row", 0, 0, tiled=True)
    grad_blocks = summed(keep, received[1], from_side)
    grad_tokens = summed(*[feature_parts[i] for i in range(feature_parts.shape[0])])
    return hidden, grad_tokens, grad_blocks[None, None]


def solution(mesh):
    in_specs = (
        P("dp", "col"),
        P("row", "col", None, None, None),
        P("row", "col", None, None),
        P("row", "col"),
        P("dp", ("row", "col")),
    )
    out_specs = (
        P("dp", ("row", "col")),
        P("dp", ("col", "row")),
        P("row", "col", "dp", None, None),
    )
    return jax.shard_map(local, mesh=mesh, in_specs=in_specs, out_specs=out_specs, check_vma=False)
```

time: 105 us -> 97.7 us (0.930)
  the two profiles are of different devices: /device:TPU:1 before, /device:TPU:24 now
where the time goes in v2:
time: 97.7 us; the launch traced here: 96.8 us
  starting transfers between devices  56.9 us (58%)
  waiting for transfers between devices  27.3 us (28%)
  Pallas kernels  5.42 us (6%)
  local copies, waits for them, and re-layouts  3.44 us (4%)
  other arithmetic  2.38 us (2%)
  between operations  1.41 us (1%)
    ppermute x4, starting transfers between devices, shifted(): return lax.ppermute(x, axis, [(i, (i + by) % n) for i in range(n)])  17.6 us
    all_to_all x1, starting transfers between devices, local(): lax.all_to_all(copies, 'col', 0, 0, tiled=True, axis_index_groups=strided)  15.2 us
    all_to_all x1, waiting for transfers between devices, local(): lax.all_to_all(hidden_near, 'col', 0, 0, tiled=True, axis_index_groups=st...  9.98 us
    all_to_all x1, starting transfers between devices, local(): lax.all_to_all(hidden_near, 'col', 0, 0, tiled=True, axis_index_groups=st...  8.11 us
    ppermute x4, waiting for transfers between devices, shifted(): return lax.ppermute(x, axis, [(i, (i + by) % n) for i in range(n)])  7.94 us
    ppermute x2, starting transfers between devices, swapped(): lax.ppermute(x, axis, [(i, i ^ bit) for i in range(lax.axis_size(axis))])  6.28 us
    all_to_all x1, starting transfers between devices, local(): feature_parts = lax.all_to_all(features, 'row', 0, 0, tiled=True)  5.76 us
    all_to_all x1, waiting for transfers between devices, local(): feature_parts = lax.all_to_all(features, 'row', 0, 0, tiled=True)  5.58 us
  transfers between devices with their start and end apart: 11, of which 5 were waited for; matrix products, arithmetic and copies ran while one was open for 2% of the time, Pallas kernels for 6%

profile of v2, /device:TPU:24, one launch (start us, length us, event | category | flops | bytes accessed | tf_op | source)
XLA Modules:
  0.0 96.8 jit_solution(7236492780780805735)
XLA Ops:
  0.6 1.5 %broadcast_in_dim.4 = bf16[4,128,256]{2,1,0:T(8,128)(2,1)} broadcast(bf16[128,256]{1,0:T(8,128)(2,1)} %param.9), dimensions={1,2} | broadcast | bytes 327680 | tf_op jit(solution)/shard_map/broadcast_in_dim | solution.py:169
  2.2 15.2 %all-to-all-start = ((bf16[4,128,256]{2,1,0:T(8,128)(2,1)}), bf16[4,128,256]{2,1,0:T(8,128)(2,1)S(1)}, u32[]{:S(2)}, u32[]{:S(2)}) async-start(bf16[4,128,256]{2,1,0:T(8,128)(2,1)} %broadcast_in_dim.4), calls=%async_computation | async-start | bytes 524288 | tf_op jit(solution)/shard_map/all_to_all | solution.py:170
  18.0 0.0 copy-start.3
  18.1 0.7 copy-done.3
  18.7 1.2 %copy-done = bf16[1,1,32,128,128]{4,3,2,1,0:T(8,128)(2,1)S(1)} copy-done((bf16[1,1,32,128,128]{4,3,2,1,0:T(8,128)(2,1)S(1)}, bf16[1,1,32,128,128]{4,3,2,1,0:T(8,128)(2,1)}, u32[]{:S(2)}) %copy-start) | copy-done | bytes 1048600
  20.0 1.6 %shard_map.76 = (bf16[4,128,256]{2,1,0:T(8,128)(2,1)S(1)}, bf16[4,128,256]{2,1,0:T(8,128)(2,1)S(1)}, bf16[4,128,256]{2,1,0:T(8,128)(2,1)S(1)}, bf16[4,128,256]{2,1,0:T(8,128)(2,1)S(1)}) custom-call(s32[2,32]{1,0:T(2,128)S(1)} %bitcast.20, s32[1,1]{1,0:T(1,128)S(6)} %copy.8.live_count, s32[1,1]{1,0:T(1,128)} %bitcast.1.plane, s32[1,1]{1,0:T(1,128)} %bitcast.2.dp_place, ...), custom_call_target="tpu_custom_call" | custom-call | flops 134217728 | bytes 524288 | tf_op jit(solution)/shard_map/pallas_call | solution.py:98
  21.5 2.9 %collective-permute-start = (bf16[4,128,256]{2,1,0:T(8,128)(2,1)S(1)}, bf16[4,128,256]{2,1,0:T(8,128)(2,1)S(1)}, u32[]{:S(2)}, u32[]{:S(2)}) collective-permute-start(bf16[4,128,256]{2,1,0:T(8,128)(2,1)S(1)} %get-tuple-element.16), channel_id=1, source_target_pairs={{0,4},{4,8},{8,12},{12,16},{16,20},{20,24},{24,28},{28,32},{32,36}... | collective-permute-start | bytes 786440 | tf_op jit(solution)/shard_map/ppermute | solution.py:130
  24.5 5.5 %collective-permute-start.1 = (bf16[4,128,256]{2,1,0:T(8,128)(2,1)S(1)}, bf16[4,128,256]{2,1,0:T(8,128)(2,1)S(1)}, u32[]{:S(2)}, u32[]{:S(2)}) collective-permute-start(bf16[4,128,256]{2,1,0:T(8,128)(2,1)S(1)} %get-tuple-element.17), channel_id=1, source_target_pairs={{0,60},{4,0},{8,4},{12,8},{16,12},{20,16},{24,20},{28,24},{32,28},... | collective-permute-start | bytes 786440 | tf_op jit(solution)/shard_map/ppermute | solution.py:130
  30.0 1.9 %collective-permute-start.2 = (bf16[4,128,256]{2,1,0:T(8,128)(2,1)S(1)}, bf16[4,128,256]{2,1,0:T(8,128)(2,1)S(1)}, u32[]{:S(2)}, u32[]{:S(2)}) collective-permute-start(bf16[4,128,256]{2,1,0:T(8,128)(2,1)S(1)} %get-tuple-element.18), channel_id=1, source_target_pairs={{0,8},{1,57},{2,10},{3,59},{4,12},{5,61},{6,14},{7,63},{8,16},{9,1... | collective-permute-start | bytes 786440 | tf_op jit(solution)/shard_map/ppermute | solution.py:140
  31.9 7.3 %collective-permute-done = bf16[4,128,256]{2,1,0:T(8,128)(2,1)S(1)} collective-permute-done((bf16[4,128,256]{2,1,0:T(8,128)(2,1)S(1)}, bf16[4,128,256]{2,1,0:T(8,128)(2,1)S(1)}, u32[]{:S(2)}, u32[]{:S(2)}) %collective-permute-start) | collective-permute-done | bytes 262176 | tf_op jit(solution)/shard_map/ppermute | solution.py:130
  39.2 0.6 collective-permute-done.1
  39.9 3.8 %collective-permute-done.2 = bf16[4,128,256]{2,1,0:T(8,128)(2,1)S(1)} collective-permute-done((bf16[4,128,256]{2,1,0:T(8,128)(2,1)S(1)}, bf16[4,128,256]{2,1,0:T(8,128)(2,1)S(1)}, u32[]{:S(2)}, u32[]{:S(2)}) %collective-permute-start.2) | collective-permute-done | bytes 262176 | tf_op jit(solution)/shard_map/ppermute | solution.py:140
  43.6 0.8 add_convert_fusion
  44.5 0.0 all-to-all-done.own
  44.5 2.0 %collective-permute-start.5 = (bf16[4,128,256]{2,1,0:T(8,128)(2,1)S(1)}, bf16[4,128,256]{2,1,0:T(8,128)(2,1)S(1)}, u32[]{:S(2)}, u32[]{:S(2)}) collective-permute-start(bf16[4,128,256]{2,1,0:T(8,128)(2,1)S(1)} %all-to-all-done.own), channel_id=1, source_target_pairs={{0,8},{1,57},{2,10},{3,59},{4,12},{5,61},{6,14},{7,63},{8,16},{9,1... | collective-permute-start | bytes 786440 | tf_op jit(solution)/shard_map/ppermute | solution.py:140
  46.5 5.1 %collective-permute-start.4 = (bf16[4,128,256]{2,1,0:T(8,128)(2,1)S(1)}, bf16[4,128,256]{2,1,0:T(8,128)(2,1)S(1)}, u32[]{:S(2)}, u32[]{:S(2)}) collective-permute-start(bf16[4,128,256]{2,1,0:T(8,128)(2,1)S(1)} %all-to-all-done.own), channel_id=1, source_target_pairs={{0,4},{4,8},{8,12},{12,16},{16,20},{20,24},{24,28},{28,32},{32,36}... | collective-permute-start | bytes 786440 | tf_op jit(solution)/shard_map/ppermute | solution.py:130
  51.7 4.0 %collective-permute-start.3 = (bf16[4,128,256]{2,1,0:T(8,128)(2,1)S(1)}, bf16[4,128,256]{2,1,0:T(8,128)(2,1)S(1)}, u32[]{:S(2)}, u32[]{:S(2)}) collective-permute-start(bf16[4,128,256]{2,1,0:T(8,128)(2,1)S(1)} %all-to-all-done.own), channel_id=1, source_target_pairs={{0,60},{4,0},{8,4},{12,8},{16,12},{20,16},{24,20},{28,24},{32,28},... | collective-permute-start | bytes 786440 | tf_op jit(solution)/shard_map/ppermute | solution.py:130
  55.7 8.1 %all-to-all-start.1 = ((bf16[4,128,256]{2,1,0:T(8,128)(2,1)}), bf16[4,128,256]{2,1,0:T(8,128)(2,1)S(1)}, u32[]{:S(2)}, u32[]{:S(2)}) async-start(bf16[4,128,256]{2,1,0:T(8,128)(2,1)} %add_convert_fusion), calls=%async_computation.1 | async-start | bytes 524288 | tf_op jit(solution)/shard_map/all_to_all | solution.py:183
  63.8 0.0 collective-permute-done.4.below
  63.8 1.2 %shard_map.78 = (bf16[8,128,128]{2,1,0:T(8,128)(2,1)S(1)}, bf16[8,128,128]{2,1,0:T(8,128)(2,1)S(1)}, bf16[2,8,128,128]{3,2,1,0:T(8,128)(2,1)S(1)}) custom-call(s32[2,32]{1,0:T(2,128)S(1)} %bitcast.21, s32[1,1]{1,0:T(1,128)S(6)} %copy.8.live_count, s32[1,1]{1,0:T(1,128)} %bitcast.1.plane, s32[1,1]{1,0:T(1,128)} %bitcast.2.dp_place, ...), custom_call_target="tpu_custom_call" | custom-call | flops 1000 | bytes 3 | tf_op jit(solution)/shard_map/pallas_call | solution.py:98
  65.1 3.1 %collective-permute-start.6 = (bf16[2,8,128,128]{3,2,1,0:T(8,128)(2,1)S(1)}, bf16[2,8,128,128]{3,2,1,0:T(8,128)(2,1)S(1)}, u32[]{:S(2)}, u32[]{:S(2)}) collective-permute-start(bf16[2,8,128,128]{3,2,1,0:T(8,128)(2,1)S(1)} %get-tuple-element.21), channel_id=1, source_target_pairs={{0,1},{1,0},{2,3},{3,2},{4,5},{5,4},{6,7},{7,6},{8,9},{9,8},{10,11... | collective-permute-start | bytes 1572872 | tf_op jit(solution)/shard_map/ppermute | solution.py:144
  68.2 1.9 %shard_map.77 = bf16[8,128,128]{2,1,0:T(8,128)(2,1)} custom-call(s32[2,32]{1,0:T(2,128)S(1)} %bitcast.22, s32[1,1]{1,0:T(1,128)S(6)} %copy.8.live_count, s32[1,1]{1,0:T(1,128)} %bitcast.1.plane, s32[1,1]{1,0:T(1,128)} %bitcast.2.dp_place, bf16[128,1024]{1,0:T(8,128)(2,1)S(1)} %copy-done.2, bf16[32,128,128]{2,1,0:T(8,128)(2,1)S(1)} %bitcast.19, ...), custom_call_target="tpu_custom_call" | custom-call | flops 1000 | bytes 3 | tf_op jit(solution)/shard_map/pallas_call | solution.py:98
  70.2 0.0 collective-permute-done.6
  70.2 0.1 fusion.2
  70.2 3.1 %collective-permute-start.7 = (bf16[8,128,128]{2,1,0:T(8,128)(2,1)S(1)}, bf16[8,128,128]{2,1,0:T(8,128)(2,1)S(1)}, u32[]{:S(2)}, u32[]{:S(2)}) collective-permute-start(bf16[8,128,128]{2,1,0:T(8,128)(2,1)S(1)} %fusion.2), channel_id=1, source_target_pairs={{0,2},{1,3},{2,0},{3,1},{4,6},{5,7},{6,4},{7,5},{8,10},{9,11},{10,... | collective-permute-start | bytes 786440 | tf_op jit(solution)/shard_map/ppermute | solution.py:144
  73.4 10.0 %all-to-all-done.1.parts = bf16[4,128,256]{2,1,0:T(8,128)(2,1)S(1)} async-done(((bf16[4,128,256]{2,1,0:T(8,128)(2,1)}), bf16[4,128,256]{2,1,0:T(8,128)(2,1)S(1)}, u32[]{:S(2)}, u32[]{:S(2)}) %all-to-all-start.1) | async-done | bytes 262176 | tf_op jit(solution)/shard_map/all_to_all | solution.py:183
  83.4 0.7 shard_map.79
  84.0 0.0 collective-permute-done.7
  84.0 5.8 %all-to-all-start.2 = ((bf16[8,128,128]{2,1,0:T(8,128)(2,1)}), bf16[8,128,128]{2,1,0:T(8,128)(2,1)S(1)}, u32[]{:S(2)}, u32[]{:S(2)}) async-start(bf16[8,128,128]{2,1,0:T(8,128)(2,1)} %shard_map.77), calls=%async_computation.2 | async-start | bytes 524288 | tf_op jit(solution)/shard_map/all_to_all | solution.py:208
  89.8 0.8 fusion.3
  90.6 5.6 %all-to-all-done.2 = bf16[8,128,128]{2,1,0:T(8,128)(2,1)S(1)} async-done(((bf16[8,128,128]{2,1,0:T(8,128)(2,1)}), bf16[8,128,128]{2,1,0:T(8,128)(2,1)S(1)}, u32[]{:S(2)}, u32[]{:S(2)}) %all-to-all-start.2) | async-done | bytes 262176 | tf_op jit(solution)/shard_map/all_to_all | solution.py:208
  96.2 0.7 fusion.4
  (7 shorter events, 0.0 us)
Async XLA Ops:
  2.2 15.9 %copy-start.2 = (bf16[128,1024]{1,0:T(8,128)(2,1)S(1)}, bf16[128,1024]{1,0:T(8,128)(2,1)}, u32[]{:S(2)}) copy-start(bf16[128,1024]{1,0:T(8,128)(2,1)} %tokens.5) | copy-start | bytes 786436
  2.2 42.3 %all-to-all-start = ((bf16[4,128,256]{2,1,0:T(8,128)(2,1)}), bf16[4,128,256]{2,1,0:T(8,128)(2,1)S(1)}, u32[]{:S(2)}, u32[]{:S(2)}) async-start(bf16[4,128,256]{2,1,0:T(8,128)(2,1)} %broadcast_in_dim.4), calls=%async_computation | async-start | bytes 524288 | tf_op jit(solution)/shard_map/all_to_all | solution.py:170
  18.0 0.7 copy-start.3
  18.7 1.2 %copy-start = (bf16[1,1,32,128,128]{4,3,2,1,0:T(8,128)(2,1)S(1)}, bf16[1,1,32,128,128]{4,3,2,1,0:T(8,128)(2,1)}, u32[]{:S(2)}) copy-start(bf16[1,1,32,128,128]{4,3,2,1,0:T(8,128)(2,1)} %param.6) | copy-start | bytes 3145732
  21.5 17.7 %collective-permute-start = (bf16[4,128,256]{2,1,0:T(8,128)(2,1)S(1)}, bf16[4,128,256]{2,1,0:T(8,128)(2,1)S(1)}, u32[]{:S(2)}, u32[]{:S(2)}) collective-permute-start(bf16[4,128,256]{2,1,0:T(8,128)(2,1)S(1)} %get-tuple-element.16), channel_id=1, source_target_pairs={{0,4},{4,8},{8,12},{12,16},{16,20},{20,24},{24,28},{28,32},{32,36}... | collective-permute-start | bytes 786440 | tf_op jit(solution)/shard_map/ppermute | solution.py:130
  24.5 15.4 %collective-permute-start.1 = (bf16[4,128,256]{2,1,0:T(8,128)(2,1)S(1)}, bf16[4,128,256]{2,1,0:T(8,128)(2,1)S(1)}, u32[]{:S(2)}, u32[]{:S(2)}) collective-permute-start(bf16[4,128,256]{2,1,0:T(8,128)(2,1)S(1)} %get-tuple-element.17), channel_id=1, source_target_pairs={{0,60},{4,0},{8,4},{12,8},{16,12},{20,16},{24,20},{28,24},{32,28},... | collective-permute-start | bytes 786440 | tf_op jit(solution)/shard_map/ppermute | solution.py:130
  30.0 13.7 %collective-permute-start.2 = (bf16[4,128,256]{2,1,0:T(8,128)(2,1)S(1)}, bf16[4,128,256]{2,1,0:T(8,128)(2,1)S(1)}, u32[]{:S(2)}, u32[]{:S(2)}) collective-permute-start(bf16[4,128,256]{2,1,0:T(8,128)(2,1)S(1)} %get-tuple-element.18), channel_id=1, source_target_pairs={{0,8},{1,57},{2,10},{3,59},{4,12},{5,61},{6,14},{7,63},{8,16},{9,1... | collective-permute-start | bytes 786440 | tf_op jit(solution)/shard_map/ppermute | solution.py:140
  44.5 23.7 %copy-start.1 = (bf16[1,1,32,128,128]{4,3,2,1,0:T(8,128)(2,1)S(1)}, bf16[1,1,32,128,128]{4,3,2,1,0:T(8,128)(2,1)}, u32[]{:S(2)}) copy-start(bf16[1,1,32,128,128]{4,3,2,1,0:T(8,128)(2,1)} %param.6) | copy-start | bytes 3145732
  44.5 19.3 %collective-permute-start.5 = (bf16[4,128,256]{2,1,0:T(8,128)(2,1)S(1)}, bf16[4,128,256]{2,1,0:T(8,128)(2,1)S(1)}, u32[]{:S(2)}, u32[]{:S(2)}) collective-permute-start(bf16[4,128,256]{2,1,0:T(8,128)(2,1)S(1)} %all-to-all-done.own), channel_id=1, source_target_pairs={{0,8},{1,57},{2,10},{3,59},{4,12},{5,61},{6,14},{7,63},{8,16},{9,1... | collective-permute-start | bytes 786440 | tf_op jit(solution)/shard_map/ppermute | solution.py:140
  46.5 17.3 %collective-permute-start.4 = (bf16[4,128,256]{2,1,0:T(8,128)(2,1)S(1)}, bf16[4,128,256]{2,1,0:T(8,128)(2,1)S(1)}, u32[]{:S(2)}, u32[]{:S(2)}) collective-permute-start(bf16[4,128,256]{2,1,0:T(8,128)(2,1)S(1)} %all-to-all-done.own), channel_id=1, source_target_pairs={{0,4},{4,8},{8,12},{12,16},{16,20},{20,24},{24,28},{28,32},{32,36}... | collective-permute-start | bytes 786440 | tf_op jit(solution)/shard_map/ppermute | solution.py:130
  51.7 12.1 %collective-permute-start.3 = (bf16[4,128,256]{2,1,0:T(8,128)(2,1)S(1)}, bf16[4,128,256]{2,1,0:T(8,128)(2,1)S(1)}, u32[]{:S(2)}, u32[]{:S(2)}) collective-permute-start(bf16[4,128,256]{2,1,0:T(8,128)(2,1)S(1)} %all-to-all-done.own), channel_id=1, source_target_pairs={{0,60},{4,0},{8,4},{12,8},{16,12},{20,16},{24,20},{28,24},{32,28},... | collective-permute-start | bytes 786440 | tf_op jit(solution)/shard_map/ppermute | solution.py:130
  55.7 27.7 %all-to-all-start.1 = ((bf16[4,128,256]{2,1,0:T(8,128)(2,1)}), bf16[4,128,256]{2,1,0:T(8,128)(2,1)S(1)}, u32[]{:S(2)}, u32[]{:S(2)}) async-start(bf16[4,128,256]{2,1,0:T(8,128)(2,1)} %add_convert_fusion), calls=%async_computation.1 | async-start | bytes 524288 | tf_op jit(solution)/shard_map/all_to_all | solution.py:183
  65.1 5.1 %collective-permute-start.6 = (bf16[2,8,128,128]{3,2,1,0:T(8,128)(2,1)S(1)}, bf16[2,8,128,128]{3,2,1,0:T(8,128)(2,1)S(1)}, u32[]{:S(2)}, u32[]{:S(2)}) collective-permute-start(bf16[2,8,128,128]{3,2,1,0:T(8,128)(2,1)S(1)} %get-tuple-element.21), channel_id=1, source_target_pairs={{0,1},{1,0},{2,3},{3,2},{4,5},{5,4},{6,7},{7,6},{8,9},{9,8},{10,11... | collective-permute-start | bytes 1572872 | tf_op jit(solution)/shard_map/ppermute | solution.py:144
  70.2 13.8 %collective-permute-start.7 = (bf16[8,128,128]{2,1,0:T(8,128)(2,1)S(1)}, bf16[8,128,128]{2,1,0:T(8,128)(2,1)S(1)}, u32[]{:S(2)}, u32[]{:S(2)}) collective-permute-start(bf16[8,128,128]{2,1,0:T(8,128)(2,1)S(1)} %fusion.2), channel_id=1, source_target_pairs={{0,2},{1,3},{2,0},{3,1},{4,6},{5,7},{6,4},{7,5},{8,10},{9,11},{10,... | collective-permute-start | bytes 786440 | tf_op jit(solution)/shard_map/ppermute | solution.py:144
  84.0 12.1 %all-to-all-start.2 = ((bf16[8,128,128]{2,1,0:T(8,128)(2,1)}), bf16[8,128,128]{2,1,0:T(8,128)(2,1)S(1)}, u32[]{:S(2)}, u32[]{:S(2)}) async-start(bf16[8,128,128]{2,1,0:T(8,128)(2,1)} %shard_map.77), calls=%async_computation.2 | async-start | bytes 524288 | tf_op jit(solution)/shard_map/all_to_all | solution.py:208

commit v3 on v2

--- a/solution.py
+++ b/solution.py
@@ -178,8 +178,10 @@
     from_below = shifted(up, "col", 1)
     from_above = shifted(down, "col", -1)
     from_far = both_ways(far, 2)
+    grads_own, from_below, from_above, from_far = lax.optimization_barrier(
+        (grads_own, from_below, from_above, from_far)
+    )
     hidden_near = summed(own, from_below, from_above, from_far)
-    grads_own, hidden_near = lax.optimization_barrier((grads_own, hidden_near))
     hidden_parts = lax.all_to_all(hidden_near, "col", 0, 0, tiled=True, axis_index_groups=strided)
     above = shifted(grads_own, "col", -1)
     below = shifted(grads_own, "col", 1)

time: 97.7 us -> 97.7 us (level)
  no operation moved by 1% of the time
where the time goes in v3:
time: 97.7 us; the launch traced here: 96.8 us
  starting transfers between devices  56.9 us (58%)
  waiting for transfers between devices  27.3 us (28%)
  Pallas kernels  5.43 us (6%)
  local copies, waits for them, and re-layouts  3.46 us (4%)
  other arithmetic  2.37 us (2%)
  between operations  1.41 us (1%)
    ppermute x4, starting transfers between devices, shifted(): return lax.ppermute(x, axis, [(i, (i + by) % n) for i in range(n)])  17.6 us
    all_to_all x1, starting transfers between devices, local(): lax.all_to_all(copies, 'col', 0, 0, tiled=True, axis_index_groups=strided)  15.2 us
    all_to_all x1, waiting for transfers between devices, local(): lax.all_to_all(hidden_near, 'col', 0, 0, tiled=True, axis_index_groups=st...  9.98 us
    all_to_all x1, starting transfers between devices, local(): lax.all_to_all(hidden_near, 'col', 0, 0, tiled=True, axis_index_groups=st...  8.23 us
    ppermute x4, waiting for transfers between devices, shifted(): return lax.ppermute(x, axis, [(i, (i + by) % n) for i in range(n)])  7.94 us
    ppermute x2, starting transfers between devices, swapped(): lax.ppermute(x, axis, [(i, i ^ bit) for i in range(lax.axis_size(axis))])  6.27 us
    all_to_all x1, starting transfers between devices, local(): feature_parts = lax.all_to_all(features, 'row', 0, 0, tiled=True)  5.76 us
    all_to_all x1, waiting for transfers between devices, local(): feature_parts = lax.all_to_all(features, 'row', 0, 0, tiled=True)  5.58 us
  transfers between devices with their start and end apart: 11, of which 5 were waited for; matrix products, arithmetic and copies ran while one was open for 2% of the time, Pallas kernels for 6%

profile of v3, /device:TPU:24, one launch (start us, length us, event | category | flops | bytes accessed | tf_op | source)
XLA Modules:
  0.0 96.8 jit_solution(7040119103204945765)
XLA Ops:
  0.6 1.6 %broadcast_in_dim.4 = bf16[4,128,256]{2,1,0:T(8,128)(2,1)} broadcast(bf16[128,256]{1,0:T(8,128)(2,1)} %param.9), dimensions={1,2} | broadcast | bytes 327680 | tf_op jit(solution)/shard_map/broadcast_in_dim | solution.py:169
  2.2 15.2 %all-to-all-start = ((bf16[4,128,256]{2,1,0:T(8,128)(2,1)}), bf16[4,128,256]{2,1,0:T(8,128)(2,1)S(1)}, u32[]{:S(2)}, u32[]{:S(2)}) async-start(bf16[4,128,256]{2,1,0:T(8,128)(2,1)} %broadcast_in_dim.4), calls=%async_computation | async-start | bytes 524288 | tf_op jit(solution)/shard_map/all_to_all | solution.py:170
  18.1 0.0 copy-start.3
  18.1 0.7 copy-done.3
  18.7 1.2 %copy-done = bf16[1,1,32,128,128]{4,3,2,1,0:T(8,128)(2,1)S(1)} copy-done((bf16[1,1,32,128,128]{4,3,2,1,0:T(8,128)(2,1)S(1)}, bf16[1,1,32,128,128]{4,3,2,1,0:T(8,128)(2,1)}, u32[]{:S(2)}) %copy-start) | copy-done | bytes 1048600
  20.0 1.6 %shard_map.76 = (bf16[4,128,256]{2,1,0:T(8,128)(2,1)S(1)}, bf16[4,128,256]{2,1,0:T(8,128)(2,1)S(1)}, bf16[4,128,256]{2,1,0:T(8,128)(2,1)S(1)}, bf16[4,128,256]{2,1,0:T(8,128)(2,1)S(1)}) custom-call(s32[2,32]{1,0:T(2,128)S(1)} %bitcast.20, s32[1,1]{1,0:T(1,128)S(6)} %copy.8.live_count, s32[1,1]{1,0:T(1,128)} %bitcast.1.plane, s32[1,1]{1,0:T(1,128)} %bitcast.2.dp_place, ...), custom_call_target="tpu_custom_call" | custom-call | flops 134217728 | bytes 524288 | tf_op jit(solution)/shard_map/pallas_call | solution.py:98
  21.6 2.9 %collective-permute-start = (bf16[4,128,256]{2,1,0:T(8,128)(2,1)S(1)}, bf16[4,128,256]{2,1,0:T(8,128)(2,1)S(1)}, u32[]{:S(2)}, u32[]{:S(2)}) collective-permute-start(bf16[4,128,256]{2,1,0:T(8,128)(2,1)S(1)} %get-tuple-element.17), channel_id=1, source_target_pairs={{0,4},{4,8},{8,12},{12,16},{16,20},{20,24},{24,28},{28,32},{32,36}... | collective-permute-start | bytes 786440 | tf_op jit(solution)/shard_map/ppermute | solution.py:130
  24.5 5.5 %collective-permute-start.1 = (bf16[4,128,256]{2,1,0:T(8,128)(2,1)S(1)}, bf16[4,128,256]{2,1,0:T(8,128)(2,1)S(1)}, u32[]{:S(2)}, u32[]{:S(2)}) collective-permute-start(bf16[4,128,256]{2,1,0:T(8,128)(2,1)S(1)} %get-tuple-element.18), channel_id=1, source_target_pairs={{0,60},{4,0},{8,4},{12,8},{16,12},{20,16},{24,20},{28,24},{32,28},... | collective-permute-start | bytes 786440 | tf_op jit(solution)/shard_map/ppermute | solution.py:130
  30.0 1.9 %collective-permute-start.2 = (bf16[4,128,256]{2,1,0:T(8,128)(2,1)S(1)}, bf16[4,128,256]{2,1,0:T(8,128)(2,1)S(1)}, u32[]{:S(2)}, u32[]{:S(2)}) collective-permute-start(bf16[4,128,256]{2,1,0:T(8,128)(2,1)S(1)} %get-tuple-element.19), channel_id=1, source_target_pairs={{0,8},{1,57},{2,10},{3,59},{4,12},{5,61},{6,14},{7,63},{8,16},{9,1... | collective-permute-start | bytes 786440 | tf_op jit(solution)/shard_map/ppermute | solution.py:140
  31.9 7.3 %collective-permute-done = bf16[4,128,256]{2,1,0:T(8,128)(2,1)S(1)} collective-permute-done((bf16[4,128,256]{2,1,0:T(8,128)(2,1)S(1)}, bf16[4,128,256]{2,1,0:T(8,128)(2,1)S(1)}, u32[]{:S(2)}, u32[]{:S(2)}) %collective-permute-start) | collective-permute-done | bytes 262176 | tf_op jit(solution)/shard_map/ppermute | solution.py:130
  39.2 0.6 collective-permute-done.1
  39.9 3.8 %collective-permute-done.2 = bf16[4,128,256]{2,1,0:T(8,128)(2,1)S(1)} collective-permute-done((bf16[4,128,256]{2,1,0:T(8,128)(2,1)S(1)}, bf16[4,128,256]{2,1,0:T(8,128)(2,1)S(1)}, u32[]{:S(2)}, u32[]{:S(2)}) %collective-permute-start.2) | collective-permute-done | bytes 262176 | tf_op jit(solution)/shard_map/ppermute | solution.py:140
  43.7 0.0 all-to-all-done.own
  43.7 1.9 %collective-permute-start.5 = (bf16[4,128,256]{2,1,0:T(8,128)(2,1)S(1)}, bf16[4,128,256]{2,1,0:T(8,128)(2,1)S(1)}, u32[]{:S(2)}, u32[]{:S(2)}) collective-permute-start(bf16[4,128,256]{2,1,0:T(8,128)(2,1)S(1)} %all-to-all-done.own), channel_id=1, source_target_pairs={{0,8},{1,57},{2,10},{3,59},{4,12},{5,61},{6,14},{7,63},{8,16},{9,1... | collective-permute-start | bytes 786440 | tf_op jit(solution)/shard_map/ppermute | solution.py:140
  45.6 5.2 %collective-permute-start.4 = (bf16[4,128,256]{2,1,0:T(8,128)(2,1)S(1)}, bf16[4,128,256]{2,1,0:T(8,128)(2,1)S(1)}, u32[]{:S(2)}, u32[]{:S(2)}) collective-permute-start(bf16[4,128,256]{2,1,0:T(8,128)(2,1)S(1)} %all-to-all-done.own), channel_id=1, source_target_pairs={{0,4},{4,8},{8,12},{12,16},{16,20},{20,24},{24,28},{28,32},{32,36}... | collective-permute-start | bytes 786440 | tf_op jit(solution)/shard_map/ppermute | solution.py:130
  50.7 4.0 %collective-permute-start.3 = (bf16[4,128,256]{2,1,0:T(8,128)(2,1)S(1)}, bf16[4,128,256]{2,1,0:T(8,128)(2,1)S(1)}, u32[]{:S(2)}, u32[]{:S(2)}) collective-permute-start(bf16[4,128,256]{2,1,0:T(8,128)(2,1)S(1)} %all-to-all-done.own), channel_id=1, source_target_pairs={{0,60},{4,0},{8,4},{12,8},{16,12},{20,16},{24,20},{28,24},{32,28},... | collective-permute-start | bytes 786440 | tf_op jit(solution)/shard_map/ppermute | solution.py:130
  54.7 0.8 add_convert_fusion
  55.6 8.2 %all-to-all-start.1 = ((bf16[4,128,256]{2,1,0:T(8,128)(2,1)}), bf16[4,128,256]{2,1,0:T(8,128)(2,1)S(1)}, u32[]{:S(2)}, u32[]{:S(2)}) async-start(bf16[4,128,256]{2,1,0:T(8,128)(2,1)} %add_convert_fusion), calls=%async_computation.1 | async-start | bytes 524288 | tf_op jit(solution)/shard_map/all_to_all | solution.py:185
  63.8 0.0 collective-permute-done.5.far
  63.8 0.0 collective-permute-done.4.below
  63.8 1.2 %shard_map.78 = (bf16[8,128,128]{2,1,0:T(8,128)(2,1)S(1)}, bf16[8,128,128]{2,1,0:T(8,128)(2,1)S(1)}, bf16[2,8,128,128]{3,2,1,0:T(8,128)(2,1)S(1)}) custom-call(s32[2,32]{1,0:T(2,128)S(1)} %bitcast.21, s32[1,1]{1,0:T(1,128)S(6)} %copy.8.live_count, s32[1,1]{1,0:T(1,128)} %bitcast.1.plane, s32[1,1]{1,0:T(1,128)} %bitcast.2.dp_place, ...), custom_call_target="tpu_custom_call" | custom-call | flops 1000 | bytes 3 | tf_op jit(solution)/shard_map/pallas_call | solution.py:98
  65.1 3.1 %collective-permute-start.6 = (bf16[2,8,128,128]{3,2,1,0:T(8,128)(2,1)S(1)}, bf16[2,8,128,128]{3,2,1,0:T(8,128)(2,1)S(1)}, u32[]{:S(2)}, u32[]{:S(2)}) collective-permute-start(bf16[2,8,128,128]{3,2,1,0:T(8,128)(2,1)S(1)} %get-tuple-element.22), channel_id=1, source_target_pairs={{0,1},{1,0},{2,3},{3,2},{4,5},{5,4},{6,7},{7,6},{8,9},{9,8},{10,11... | collective-permute-start | bytes 1572872 | tf_op jit(solution)/shard_map/ppermute | solution.py:144
  68.2 1.9 %shard_map.77 = bf16[8,128,128]{2,1,0:T(8,128)(2,1)} custom-call(s32[2,32]{1,0:T(2,128)S(1)} %bitcast.22, s32[1,1]{1,0:T(1,128)S(6)} %copy.8.live_count, s32[1,1]{1,0:T(1,128)} %bitcast.1.plane, s32[1,1]{1,0:T(1,128)} %bitcast.2.dp_place, bf16[128,1024]{1,0:T(8,128)(2,1)S(1)} %copy-done.2, bf16[32,128,128]{2,1,0:T(8,128)(2,1)S(1)} %bitcast.19, ...), custom_call_target="tpu_custom_call" | custom-call | flops 1000 | bytes 3 | tf_op jit(solution)/shard_map/pallas_call | solution.py:98
  70.2 0.0 collective-permute-done.6
  70.2 0.1 fusion.2
  70.2 3.1 %collective-permute-start.7 = (bf16[8,128,128]{2,1,0:T(8,128)(2,1)S(1)}, bf16[8,128,128]{2,1,0:T(8,128)(2,1)S(1)}, u32[]{:S(2)}, u32[]{:S(2)}) collective-permute-start(bf16[8,128,128]{2,1,0:T(8,128)(2,1)S(1)} %fusion.2), channel_id=1, source_target_pairs={{0,2},{1,3},{2,0},{3,1},{4,6},{5,7},{6,4},{7,5},{8,10},{9,11},{10,... | collective-permute-start | bytes 786440 | tf_op jit(solution)/shard_map/ppermute | solution.py:144
  73.4 10.0 %all-to-all-done.1.parts = bf16[4,128,256]{2,1,0:T(8,128)(2,1)S(1)} async-done(((bf16[4,128,256]{2,1,0:T(8,128)(2,1)}), bf16[4,128,256]{2,1,0:T(8,128)(2,1)S(1)}, u32[]{:S(2)}, u32[]{:S(2)}) %all-to-all-start.1) | async-done | bytes 262176 | tf_op jit(solution)/shard_map/all_to_all | solution.py:185
  83.4 0.7 shard_map.79
  84.0 5.8 %all-to-all-start.2 = ((bf16[8,128,128]{2,1,0:T(8,128)(2,1)}), bf16[8,128,128]{2,1,0:T(8,128)(2,1)S(1)}, u32[]{:S(2)}, u32[]{:S(2)}) async-start(bf16[8,128,128]{2,1,0:T(8,128)(2,1)} %shard_map.77), calls=%async_computation.2 | async-start | bytes 524288 | tf_op jit(solution)/shard_map/all_to_all | solution.py:210
  89.8 0.8 fusion.3
  90.6 5.6 %all-to-all-done.2 = bf16[8,128,128]{2,1,0:T(8,128)(2,1)S(1)} async-done(((bf16[8,128,128]{2,1,0:T(8,128)(2,1)}), bf16[8,128,128]{2,1,0:T(8,128)(2,1)S(1)}, u32[]{:S(2)}, u32[]{:S(2)}) %all-to-all-start.2) | async-done | bytes 262176 | tf_op jit(solution)/shard_map/all_to_all | solution.py:210
  96.2 0.7 fusion.4
  (7 shorter events, 0.0 us)
Async XLA Ops:
  2.2 15.9 %copy-start.2 = (bf16[128,1024]{1,0:T(8,128)(2,1)S(1)}, bf16[128,1024]{1,0:T(8,128)(2,1)}, u32[]{:S(2)}) copy-start(bf16[128,1024]{1,0:T(8,128)(2,1)} %tokens.5) | copy-start | bytes 786436
  2.2 41.5 %all-to-all-start = ((bf16[4,128,256]{2,1,0:T(8,128)(2,1)}), bf16[4,128,256]{2,1,0:T(8,128)(2,1)S(1)}, u32[]{:S(2)}, u32[]{:S(2)}) async-start(bf16[4,128,256]{2,1,0:T(8,128)(2,1)} %broadcast_in_dim.4), calls=%async_computation | async-start | bytes 524288 | tf_op jit(solution)/shard_map/all_to_all | solution.py:170
  18.1 0.7 copy-start.3
  18.7 1.2 %copy-start = (bf16[1,1,32,128,128]{4,3,2,1,0:T(8,128)(2,1)S(1)}, bf16[1,1,32,128,128]{4,3,2,1,0:T(8,128)(2,1)}, u32[]{:S(2)}) copy-start(bf16[1,1,32,128,128]{4,3,2,1,0:T(8,128)(2,1)} %param.6) | copy-start | bytes 3145732
  21.6 17.7 %collective-permute-start = (bf16[4,128,256]{2,1,0:T(8,128)(2,1)S(1)}, bf16[4,128,256]{2,1,0:T(8,128)(2,1)S(1)}, u32[]{:S(2)}, u32[]{:S(2)}) collective-permute-start(bf16[4,128,256]{2,1,0:T(8,128)(2,1)S(1)} %get-tuple-element.17), channel_id=1, source_target_pairs={{0,4},{4,8},{8,12},{12,16},{16,20},{20,24},{24,28},{28,32},{32,36}... | collective-permute-start | bytes 786440 | tf_op jit(solution)/shard_map/ppermute | solution.py:130
  24.5 15.4 %collective-permute-start.1 = (bf16[4,128,256]{2,1,0:T(8,128)(2,1)S(1)}, bf16[4,128,256]{2,1,0:T(8,128)(2,1)S(1)}, u32[]{:S(2)}, u32[]{:S(2)}) collective-permute-start(bf16[4,128,256]{2,1,0:T(8,128)(2,1)S(1)} %get-tuple-element.18), channel_id=1, source_target_pairs={{0,60},{4,0},{8,4},{12,8},{16,12},{20,16},{24,20},{28,24},{32,28},... | collective-permute-start | bytes 786440 | tf_op jit(solution)/shard_map/ppermute | solution.py:130
  30.0 13.6 %collective-permute-start.2 = (bf16[4,128,256]{2,1,0:T(8,128)(2,1)S(1)}, bf16[4,128,256]{2,1,0:T(8,128)(2,1)S(1)}, u32[]{:S(2)}, u32[]{:S(2)}) collective-permute-start(bf16[4,128,256]{2,1,0:T(8,128)(2,1)S(1)} %get-tuple-element.19), channel_id=1, source_target_pairs={{0,8},{1,57},{2,10},{3,59},{4,12},{5,61},{6,14},{7,63},{8,16},{9,1... | collective-permute-start | bytes 786440 | tf_op jit(solution)/shard_map/ppermute | solution.py:140
  43.7 20.1 %collective-permute-start.5 = (bf16[4,128,256]{2,1,0:T(8,128)(2,1)S(1)}, bf16[4,128,256]{2,1,0:T(8,128)(2,1)S(1)}, u32[]{:S(2)}, u32[]{:S(2)}) collective-permute-start(bf16[4,128,256]{2,1,0:T(8,128)(2,1)S(1)} %all-to-all-done.own), channel_id=1, source_target_pairs={{0,8},{1,57},{2,10},{3,59},{4,12},{5,61},{6,14},{7,63},{8,16},{9,1... | collective-permute-start | bytes 786440 | tf_op jit(solution)/shard_map/ppermute | solution.py:140
  45.6 18.2 %collective-permute-start.4 = (bf16[4,128,256]{2,1,0:T(8,128)(2,1)S(1)}, bf16[4,128,256]{2,1,0:T(8,128)(2,1)S(1)}, u32[]{:S(2)}, u32[]{:S(2)}) collective-permute-start(bf16[4,128,256]{2,1,0:T(8,128)(2,1)S(1)} %all-to-all-done.own), channel_id=1, source_target_pairs={{0,4},{4,8},{8,12},{12,16},{16,20},{20,24},{24,28},{28,32},{32,36}... | collective-permute-start | bytes 786440 | tf_op jit(solution)/shard_map/ppermute | solution.py:130
  50.7 13.1 %collective-permute-start.3 = (bf16[4,128,256]{2,1,0:T(8,128)(2,1)S(1)}, bf16[4,128,256]{2,1,0:T(8,128)(2,1)S(1)}, u32[]{:S(2)}, u32[]{:S(2)}) collective-permute-start(bf16[4,128,256]{2,1,0:T(8,128)(2,1)S(1)} %all-to-all-done.own), channel_id=1, source_target_pairs={{0,60},{4,0},{8,4},{12,8},{16,12},{20,16},{24,20},{28,24},{32,28},... | collective-permute-start | bytes 786440 | tf_op jit(solution)/shard_map/ppermute | solution.py:130
  55.6 12.6 %copy-start.1 = (bf16[1,1,32,128,128]{4,3,2,1,0:T(8,128)(2,1)S(1)}, bf16[1,1,32,128,128]{4,3,2,1,0:T(8,128)(2,1)}, u32[]{:S(2)}) copy-start(bf16[1,1,32,128,128]{4,3,2,1,0:T(8,128)(2,1)} %param.6) | copy-start | bytes 3145732
  55.6 27.8 %all-to-all-start.1 = ((bf16[4,128,256]{2,1,0:T(8,128)(2,1)}), bf16[4,128,256]{2,1,0:T(8,128)(2,1)S(1)}, u32[]{:S(2)}, u32[]{:S(2)}) async-start(bf16[4,128,256]{2,1,0:T(8,128)(2,1)} %add_convert_fusion), calls=%async_computation.1 | async-start | bytes 524288 | tf_op jit(solution)/shard_map/all_to_all | solution.py:185
  65.1 5.1 %collective-permute-start.6 = (bf16[2,8,128,128]{3,2,1,0:T(8,128)(2,1)S(1)}, bf16[2,8,128,128]{3,2,1,0:T(8,128)(2,1)S(1)}, u32[]{:S(2)}, u32[]{:S(2)}) collective-permute-start(bf16[2,8,128,128]{3,2,1,0:T(8,128)(2,1)S(1)} %get-tuple-element.22), channel_id=1, source_target_pairs={{0,1},{1,0},{2,3},{3,2},{4,5},{5,4},{6,7},{7,6},{8,9},{9,8},{10,11... | collective-permute-start | bytes 1572872 | tf_op jit(solution)/shard_map/ppermute | solution.py:144
  70.2 13.8 %collective-permute-start.7 = (bf16[8,128,128]{2,1,0:T(8,128)(2,1)S(1)}, bf16[8,128,128]{2,1,0:T(8,128)(2,1)S(1)}, u32[]{:S(2)}, u32[]{:S(2)}) collective-permute-start(bf16[8,128,128]{2,1,0:T(8,128)(2,1)S(1)} %fusion.2), channel_id=1, source_target_pairs={{0,2},{1,3},{2,0},{3,1},{4,6},{5,7},{6,4},{7,5},{8,10},{9,11},{10,... | collective-permute-start | bytes 786440 | tf_op jit(solution)/shard_map/ppermute | solution.py:144
  84.0 12.1 %all-to-all-start.2 = ((bf16[8,128,128]{2,1,0:T(8,128)(2,1)}), bf16[8,128,128]{2,1,0:T(8,128)(2,1)S(1)}, u32[]{:S(2)}, u32[]{:S(2)}) async-start(bf16[8,128,128]{2,1,0:T(8,128)(2,1)} %shard_map.77), calls=%async_computation.2 | async-start | bytes 524288 | tf_op jit(solution)/shard_map/all_to_all | solution.py:210

commit v4 on v3

--- a/solution.py
+++ b/solution.py
@@ -79,7 +79,7 @@
 
 def features_kernel(
     index, live_count, plane, dp_place, tokens, weights, own, above, below, far,
-    features, token_blocks, grads, total,
+    kept, sent, token_blocks, grads, total,
 ):
     gather_blocks(plane, dp_place, tokens, (own, above, below, far), token_blocks, grads)
     cols = total.shape[0] - 1
@@ -90,8 +90,10 @@
         total[jnp.where(live, index[1, s], cols)] += jnp.dot(
             grads[jnp.where(live, index[0, s], 0)], weights[s], preferred_element_type=f32
         )
-    for m in range(cols):
-        features[m] = total[m].astype(bf16)
+    here = lax.rem(dp_place[0, 1], 2)
+    for k in range(cols // 2):
+        kept[k] = total[2 * k + here].astype(bf16)
+        sent[k] = total[2 * k + 1 - here].astype(bf16)
 
 
 def call(kernel, outs, scratch, flops, *operands):
@@ -161,7 +163,7 @@
     place = lax.axis_index("col")
     dp = lax.axis_index("dp")
     quarter = (planes // 4, token_count, grad_hidden.shape[1])
-    info = (block_index[0, 0], block_count, place.reshape(1, 1), dp.reshape(1, 1))
+    info = (block_index[0, 0], block_count, place.reshape(1, 1), jnp.stack([dp, lax.axis_index("row")])[None])
     blocks = (token_count, block)
     owned = (capacity // lax.axis_size("dp"), block, block)
 
@@ -198,17 +200,22 @@
     received = swapped(send, "dp", 1)
     theirs = summed(keep_far, received[0])
     from_side = swapped(theirs, "dp", 2)
-    [features] = call(
+    kept, sent = call(
         features_kernel,
-        [(col_blocks, *blocks)],
+        [(col_blocks // 2, *blocks)] * 2,
         [token_scratch, grads_scratch, ((col_blocks + 1, *blocks), f32)],
         low_cost,
         *info, tokens, weights, grads_own, above, below, across,
     )
+    features = summed(kept, swapped(sent, "row", 1))
     hidden = call_sum(hidden_parts, high_cost)
-    features, from_side, hidden = lax.optimization_barrier((features, from_side, hidden))
-    feature_parts = lax.all_to_all(features, "row", 0, 0, tiled=True)
+    features, hidden = lax.optimization_barrier((features, hidden))
+    along_x = [list(range(i, col_blocks, 2)) for i in range(2)]
+    feature_parts = lax.all_to_all(
+        features, "row", 0, 0, tiled=True, axis_index_groups=along_x
+    )
     grad_blocks = summed(keep, received[1], from_side)
+    feature_parts, grad_blocks = lax.optimization_barrier((feature_parts, grad_blocks))
     grad_tokens = summed(*[feature_parts[i] for i in range(feature_parts.shape[0])])
     return hidden, grad_tokens, grad_blocks[None, None]
 

time: 97.7 us -> 95.7 us (0.980)
  waiting for transfers between devices: 27.3 us -> 24.2 us
  starting transfers between devices: 56.9 us -> 58 us
    all_to_all x1, waiting for transfers between devices: 9.98 us -> 2.68 us  [local(): lax.all_to_all(hidden_near, 'col', 0, 0, tiled=True, axis_index_groups=st...]
    ppermute x2 -> x3, waiting for transfers between devices: 0.01 us -> 4.65 us  [swapped(): lax.ppermute(x, axis, [(i, i ^ bit) for i in range(lax.axis_size(axis))])]
    ppermute x2 -> x3, starting transfers between devices: 6.27 us -> 8.92 us  [swapped(): lax.ppermute(x, axis, [(i, i ^ bit) for i in range(lax.axis_size(axis))])]
    all_to_all x1, starting transfers between devices: 5.76 us -> 4.29 us  [local(): lax.all_to_all(features, 'row', 0, 0, tiled=True, axis_index_groups=along_x)]
    convert_element_type x3 -> x4, other arithmetic: 1.56 us -> 2.4 us  [summed(): return total.astype(bf16)]
  transfers between devices with their start and end apart: 11 -> 12, of which waited for: 5 -> 6; matrix products, arithmetic and copies ran while one was open for 2% -> 3% of each run, Pallas kernels for 6% -> 5%
where the time goes in v4:
time: 95.7 us; the launch traced here: 94.9 us
  starting transfers between devices  58 us (61%)
  waiting for transfers between devices  24.2 us (25%)
  Pallas kernels  4.73 us (5%)
  local copies, waits for them, and re-layouts  3.47 us (4%)
  other arithmetic  3.11 us (3%)
  between operations  1.41 us (1%)
    ppermute x4, starting transfers between devices, shifted(): return lax.ppermute(x, axis, [(i, (i + by) % n) for i in range(n)])  17.5 us
    all_to_all x1, starting transfers between devices, local(): lax.all_to_all(copies, 'col', 0, 0, tiled=True, axis_index_groups=strided)  15.2 us
    ppermute x3, starting transfers between devices, swapped(): lax.ppermute(x, axis, [(i, i ^ bit) for i in range(lax.axis_size(axis))])  8.92 us
    all_to_all x1, starting transfers between devices, local(): lax.all_to_all(hidden_near, 'col', 0, 0, tiled=True, axis_index_groups=st...  8.23 us
    ppermute x4, waiting for transfers between devices, shifted(): return lax.ppermute(x, axis, [(i, (i + by) % n) for i in range(n)])  7.89 us
    all_to_all x1, waiting for transfers between devices, local(): lax.all_to_all(features, 'row', 0, 0, tiled=True, axis_index_groups=along_x)  5.16 us
    ppermute x3, waiting for transfers between devices, swapped(): lax.ppermute(x, axis, [(i, i ^ bit) for i in range(lax.axis_size(axis))])  4.65 us
    all_to_all x1, starting transfers between devices, local(): lax.all_to_all(features, 'row', 0, 0, tiled=True, axis_index_groups=along_x)  4.29 us
  transfers between devices with their start and end apart: 12, of which 6 were waited for; matrix products, arithmetic and copies ran while one was open for 3% of the time, Pallas kernels for 5%

profile of v4, /device:TPU:24, one launch (start us, length us, event | category | flops | bytes accessed | tf_op | source)
XLA Modules:
  0.0 94.9 jit_solution(16714001063150709952)
XLA Ops:
  0.6 1.6 %broadcast_in_dim.13 = bf16[4,128,256]{2,1,0:T(8,128)(2,1)} broadcast(bf16[128,256]{1,0:T(8,128)(2,1)} %param.9), dimensions={1,2} | broadcast | bytes 327680 | tf_op jit(solution)/shard_map/broadcast_in_dim | solution.py:171
  2.2 15.2 %all-to-all-start = ((bf16[4,128,256]{2,1,0:T(8,128)(2,1)}), bf16[4,128,256]{2,1,0:T(8,128)(2,1)S(1)}, u32[]{:S(2)}, u32[]{:S(2)}) async-start(bf16[4,128,256]{2,1,0:T(8,128)(2,1)} %broadcast_in_dim.13), calls=%async_computation | async-start | bytes 524288 | tf_op jit(solution)/shard_map/all_to_all | solution.py:172
  18.1 0.1 add_bitcast_fusion.dp_place
  18.1 0.7 copy-done.3
  18.8 1.2 %copy-done = bf16[1,1,32,128,128]{4,3,2,1,0:T(8,128)(2,1)S(1)} copy-done((bf16[1,1,32,128,128]{4,3,2,1,0:T(8,128)(2,1)S(1)}, bf16[1,1,32,128,128]{4,3,2,1,0:T(8,128)(2,1)}, u32[]{:S(2)}) %copy-start) | copy-done | bytes 1048600
  20.0 1.6 %shard_map.76 = (bf16[4,128,256]{2,1,0:T(8,128)(2,1)S(1)}, bf16[4,128,256]{2,1,0:T(8,128)(2,1)S(1)}, bf16[4,128,256]{2,1,0:T(8,128)(2,1)S(1)}, bf16[4,128,256]{2,1,0:T(8,128)(2,1)S(1)}) custom-call(s32[2,32]{1,0:T(2,128)S(1)} %bitcast.22, s32[1,1]{1,0:T(1,128)S(6)} %copy.8.live_count, s32[1,1]{1,0:T(1,128)} %bitcast.1.plane, ...), custom_call_target="tpu_custom_call" | custom-call | flops 134217728 | bytes 524288 | tf_op jit(solution)/shard_map/pallas_call | solution.py:100
  21.6 2.9 %collective-permute-start = (bf16[4,128,256]{2,1,0:T(8,128)(2,1)S(1)}, bf16[4,128,256]{2,1,0:T(8,128)(2,1)S(1)}, u32[]{:S(2)}, u32[]{:S(2)}) collective-permute-start(bf16[4,128,256]{2,1,0:T(8,128)(2,1)S(1)} %get-tuple-element.20), channel_id=1, source_target_pairs={{0,4},{4,8},{8,12},{12,16},{16,20},{20,24},{24,28},{28,32},{32,36}... | collective-permute-start | bytes 786440 | tf_op jit(solution)/shard_map/ppermute | solution.py:132
  24.6 5.5 %collective-permute-start.1 = (bf16[4,128,256]{2,1,0:T(8,128)(2,1)S(1)}, bf16[4,128,256]{2,1,0:T(8,128)(2,1)S(1)}, u32[]{:S(2)}, u32[]{:S(2)}) collective-permute-start(bf16[4,128,256]{2,1,0:T(8,128)(2,1)S(1)} %get-tuple-element.21), channel_id=1, source_target_pairs={{0,60},{4,0},{8,4},{12,8},{16,12},{20,16},{24,20},{28,24},{32,28},... | collective-permute-start | bytes 786440 | tf_op jit(solution)/shard_map/ppermute | solution.py:132
  30.1 1.9 %collective-permute-start.2 = (bf16[4,128,256]{2,1,0:T(8,128)(2,1)S(1)}, bf16[4,128,256]{2,1,0:T(8,128)(2,1)S(1)}, u32[]{:S(2)}, u32[]{:S(2)}) collective-permute-start(bf16[4,128,256]{2,1,0:T(8,128)(2,1)S(1)} %get-tuple-element.22), channel_id=1, source_target_pairs={{0,8},{1,57},{2,10},{3,59},{4,12},{5,61},{6,14},{7,63},{8,16},{9,1... | collective-permute-start | bytes 786440 | tf_op jit(solution)/shard_map/ppermute | solution.py:142
  32.0 7.2 %collective-permute-done = bf16[4,128,256]{2,1,0:T(8,128)(2,1)S(1)} collective-permute-done((bf16[4,128,256]{2,1,0:T(8,128)(2,1)S(1)}, bf16[4,128,256]{2,1,0:T(8,128)(2,1)S(1)}, u32[]{:S(2)}, u32[]{:S(2)}) %collective-permute-start) | collective-permute-done | bytes 262176 | tf_op jit(solution)/shard_map/ppermute | solution.py:132
  39.2 0.7 collective-permute-done.1
  39.9 3.8 %collective-permute-done.2 = bf16[4,128,256]{2,1,0:T(8,128)(2,1)S(1)} collective-permute-done((bf16[4,128,256]{2,1,0:T(8,128)(2,1)S(1)}, bf16[4,128,256]{2,1,0:T(8,128)(2,1)S(1)}, u32[]{:S(2)}, u32[]{:S(2)}) %collective-permute-start.2) | collective-permute-done | bytes 262176 | tf_op jit(solution)/shard_map/ppermute | solution.py:142
  43.7 0.0 all-to-all-done.own
  43.7 1.9 %collective-permute-start.5 = (bf16[4,128,256]{2,1,0:T(8,128)(2,1)S(1)}, bf16[4,128,256]{2,1,0:T(8,128)(2,1)S(1)}, u32[]{:S(2)}, u32[]{:S(2)}) collective-permute-start(bf16[4,128,256]{2,1,0:T(8,128)(2,1)S(1)} %all-to-all-done.own), channel_id=1, source_target_pairs={{0,8},{1,57},{2,10},{3,59},{4,12},{5,61},{6,14},{7,63},{8,16},{9,1... | collective-permute-start | bytes 786440 | tf_op jit(solution)/shard_map/ppermute | solution.py:142
  45.6 5.1 %collective-permute-start.4 = (bf16[4,128,256]{2,1,0:T(8,128)(2,1)S(1)}, bf16[4,128,256]{2,1,0:T(8,128)(2,1)S(1)}, u32[]{:S(2)}, u32[]{:S(2)}) collective-permute-start(bf16[4,128,256]{2,1,0:T(8,128)(2,1)S(1)} %all-to-all-done.own), channel_id=1, source_target_pairs={{0,4},{4,8},{8,12},{12,16},{16,20},{20,24},{24,28},{28,32},{32,36}... | collective-permute-start | bytes 786440 | tf_op jit(solution)/shard_map/ppermute | solution.py:132
  50.8 4.0 %collective-permute-start.3 = (bf16[4,128,256]{2,1,0:T(8,128)(2,1)S(1)}, bf16[4,128,256]{2,1,0:T(8,128)(2,1)S(1)}, u32[]{:S(2)}, u32[]{:S(2)}) collective-permute-start(bf16[4,128,256]{2,1,0:T(8,128)(2,1)S(1)} %all-to-all-done.own), channel_id=1, source_target_pairs={{0,60},{4,0},{8,4},{12,8},{16,12},{20,16},{24,20},{28,24},{32,28},... | collective-permute-start | bytes 786440 | tf_op jit(solution)/shard_map/ppermute | solution.py:132
  54.7 0.8 add_convert_fusion
  55.6 8.2 %all-to-all-start.1 = ((bf16[4,128,256]{2,1,0:T(8,128)(2,1)}), bf16[4,128,256]{2,1,0:T(8,128)(2,1)S(1)}, u32[]{:S(2)}, u32[]{:S(2)}) async-start(bf16[4,128,256]{2,1,0:T(8,128)(2,1)} %add_convert_fusion), calls=%async_computation.1 | async-start | bytes 524288 | tf_op jit(solution)/shard_map/all_to_all | solution.py:187
  63.8 1.2 %shard_map.79 = (bf16[8,128,128]{2,1,0:T(8,128)(2,1)S(1)}, bf16[8,128,128]{2,1,0:T(8,128)(2,1)S(1)}, bf16[2,8,128,128]{3,2,1,0:T(8,128)(2,1)S(1)}) custom-call(s32[2,32]{1,0:T(2,128)S(1)} %bitcast.23, s32[1,1]{1,0:T(1,128)S(6)} %copy.8.live_count, s32[1,1]{1,0:T(1,128)} %bitcast.1.plane, s32[1,2]{1,0:T(1,128)S(1)} %add_bitcast_fusion.dp_place, ...), custom_call_target="tpu_custom_call" | custom-call | flops 1000 | bytes 3 | tf_op jit(solution)/shard_map/pallas_call | solution.py:100
  65.1 3.1 %collective-permute-start.7 = (bf16[2,8,128,128]{3,2,1,0:T(8,128)(2,1)S(1)}, bf16[2,8,128,128]{3,2,1,0:T(8,128)(2,1)S(1)}, u32[]{:S(2)}, u32[]{:S(2)}) collective-permute-start(bf16[2,8,128,128]{3,2,1,0:T(8,128)(2,1)S(1)} %get-tuple-element.33), channel_id=1, source_target_pairs={{0,1},{1,0},{2,3},{3,2},{4,5},{5,4},{6,7},{7,6},{8,9},{9,8},{10,11... | collective-permute-start | bytes 1572872 | tf_op jit(solution)/shard_map/ppermute | solution.py:146
  68.2 1.2 %shard_map.77 = (bf16[4,128,128]{2,1,0:T(8,128)(2,1)S(1)}, bf16[4,128,128]{2,1,0:T(8,128)(2,1)S(1)}) custom-call(s32[2,32]{1,0:T(2,128)S(1)} %bitcast.24, s32[1,1]{1,0:T(1,128)S(6)} %copy.8.live_count, s32[1,1]{1,0:T(1,128)} %bitcast.1.plane, s32[1,2]{1,0:T(1,128)S(1)} %add_bitcast_fusion.dp_place, bf16[128,1024]{1,0:T(8,128)(2,1)S(1)} %copy-done.2, ...), custom_call_target="tpu_custom_call" | custom-call | flops 1000 | bytes 3 | tf_op jit(solution)/shard_map/pallas_call | solution.py:100
  69.5 2.7 %collective-permute-start.6 = (bf16[4,128,128]{2,1,0:T(8,128)(2,1)S(1)}, bf16[4,128,128]{2,1,0:T(8,128)(2,1)S(1)}, u32[]{:S(2)}, u32[]{:S(2)}) collective-permute-start(bf16[4,128,128]{2,1,0:T(8,128)(2,1)S(1)} %get-tuple-element.25), channel_id=1, source_target_pairs={{0,64},{64,0},{128,192},{192,128},{256,320},{320,256},{384,448},{4... | collective-permute-start | bytes 393224 | tf_op jit(solution)/shard_map/ppermute | solution.py:146
  72.1 4.6 %collective-permute-done.6 = bf16[4,128,128]{2,1,0:T(8,128)(2,1)S(1)} collective-permute-done((bf16[4,128,128]{2,1,0:T(8,128)(2,1)S(1)}, bf16[4,128,128]{2,1,0:T(8,128)(2,1)S(1)}, u32[]{:S(2)}, u32[]{:S(2)}) %collective-permute-start.6) | collective-permute-done | bytes 131104 | tf_op jit(solution)/shard_map/ppermute | solution.py:146
  76.8 0.7 add_convert_fusion.1
  77.5 0.1 fusion
  77.5 3.1 %collective-permute-start.8 = (bf16[8,128,128]{2,1,0:T(8,128)(2,1)S(1)}, bf16[8,128,128]{2,1,0:T(8,128)(2,1)S(1)}, u32[]{:S(2)}, u32[]{:S(2)}) collective-permute-start(bf16[8,128,128]{2,1,0:T(8,128)(2,1)S(1)} %fusion), channel_id=1, source_target_pairs={{0,2},{1,3},{2,0},{3,1},{4,6},{5,7},{6,4},{7,5},{8,10},{9,11},{10,... | collective-permute-start | bytes 786440 | tf_op jit(solution)/shard_map/ppermute | solution.py:146
  80.7 2.7 %all-to-all-done.1.parts = bf16[4,128,256]{2,1,0:T(8,128)(2,1)S(1)} async-done(((bf16[4,128,256]{2,1,0:T(8,128)(2,1)}), bf16[4,128,256]{2,1,0:T(8,128)(2,1)S(1)}, u32[]{:S(2)}, u32[]{:S(2)}) %all-to-all-start.1) | async-done | bytes 262176 | tf_op jit(solution)/shard_map/all_to_all | solution.py:187
  83.4 0.7 shard_map.78
  84.0 4.3 %all-to-all-start.2 = ((bf16[4,128,128]{2,1,0:T(8,128)(2,1)}), bf16[4,128,128]{2,1,0:T(8,128)(2,1)S(1)}, u32[]{:S(2)}, u32[]{:S(2)}) async-start(bf16[4,128,128]{2,1,0:T(8,128)(2,1)} %add_convert_fusion.1), calls=%async_computation.2 | async-start | bytes 262144 | tf_op jit(solution)/shard_map/all_to_all | solution.py:214
  88.3 0.8 fusion.2
  89.1 5.2 %all-to-all-done.2 = bf16[4,128,128]{2,1,0:T(8,128)(2,1)S(1)} async-done(((bf16[4,128,128]{2,1,0:T(8,128)(2,1)}), bf16[4,128,128]{2,1,0:T(8,128)(2,1)S(1)}, u32[]{:S(2)}, u32[]{:S(2)}) %all-to-all-start.2) | async-done | bytes 131104 | tf_op jit(solution)/shard_map/all_to_all | solution.py:214
  94.3 0.6 fusion.3
  (11 shorter events, 0.0 us)
Async XLA Ops:
  2.2 15.9 %copy-start.2 = (bf16[128,1024]{1,0:T(8,128)(2,1)S(1)}, bf16[128,1024]{1,0:T(8,128)(2,1)}, u32[]{:S(2)}) copy-start(bf16[128,1024]{1,0:T(8,128)(2,1)} %tokens.5) | copy-start | bytes 786436
  2.2 41.5 %all-to-all-start = ((bf16[4,128,256]{2,1,0:T(8,128)(2,1)}), bf16[4,128,256]{2,1,0:T(8,128)(2,1)S(1)}, u32[]{:S(2)}, u32[]{:S(2)}) async-start(bf16[4,128,256]{2,1,0:T(8,128)(2,1)} %broadcast_in_dim.13), calls=%async_computation | async-start | bytes 524288 | tf_op jit(solution)/shard_map/all_to_all | solution.py:172
  18.1 0.7 copy-start.3
  18.8 1.2 %copy-start = (bf16[1,1,32,128,128]{4,3,2,1,0:T(8,128)(2,1)S(1)}, bf16[1,1,32,128,128]{4,3,2,1,0:T(8,128)(2,1)}, u32[]{:S(2)}) copy-start(bf16[1,1,32,128,128]{4,3,2,1,0:T(8,128)(2,1)} %param.6) | copy-start | bytes 3145732
  21.6 17.6 %collective-permute-start = (bf16[4,128,256]{2,1,0:T(8,128)(2,1)S(1)}, bf16[4,128,256]{2,1,0:T(8,128)(2,1)S(1)}, u32[]{:S(2)}, u32[]{:S(2)}) collective-permute-start(bf16[4,128,256]{2,1,0:T(8,128)(2,1)S(1)} %get-tuple-element.20), channel_id=1, source_target_pairs={{0,4},{4,8},{8,12},{12,16},{16,20},{20,24},{24,28},{28,32},{32,36}... | collective-permute-start | bytes 786440 | tf_op jit(solution)/shard_map/ppermute | solution.py:132
  24.6 15.3 %collective-permute-start.1 = (bf16[4,128,256]{2,1,0:T(8,128)(2,1)S(1)}, bf16[4,128,256]{2,1,0:T(8,128)(2,1)S(1)}, u32[]{:S(2)}, u32[]{:S(2)}) collective-permute-start(bf16[4,128,256]{2,1,0:T(8,128)(2,1)S(1)} %get-tuple-element.21), channel_id=1, source_target_pairs={{0,60},{4,0},{8,4},{12,8},{16,12},{20,16},{24,20},{28,24},{32,28},... | collective-permute-start | bytes 786440 | tf_op jit(solution)/shard_map/ppermute | solution.py:132
  30.1 13.6 %collective-permute-start.2 = (bf16[4,128,256]{2,1,0:T(8,128)(2,1)S(1)}, bf16[4,128,256]{2,1,0:T(8,128)(2,1)S(1)}, u32[]{:S(2)}, u32[]{:S(2)}) collective-permute-start(bf16[4,128,256]{2,1,0:T(8,128)(2,1)S(1)} %get-tuple-element.22), channel_id=1, source_target_pairs={{0,8},{1,57},{2,10},{3,59},{4,12},{5,61},{6,14},{7,63},{8,16},{9,1... | collective-permute-start | bytes 786440 | tf_op jit(solution)/shard_map/ppermute | solution.py:142
  43.7 20.1 %collective-permute-start.5 = (bf16[4,128,256]{2,1,0:T(8,128)(2,1)S(1)}, bf16[4,128,256]{2,1,0:T(8,128)(2,1)S(1)}, u32[]{:S(2)}, u32[]{:S(2)}) collective-permute-start(bf16[4,128,256]{2,1,0:T(8,128)(2,1)S(1)} %all-to-all-done.own), channel_id=1, source_target_pairs={{0,8},{1,57},{2,10},{3,59},{4,12},{5,61},{6,14},{7,63},{8,16},{9,1... | collective-permute-start | bytes 786440 | tf_op jit(solution)/shard_map/ppermute | solution.py:142
  45.6 18.2 %collective-permute-start.4 = (bf16[4,128,256]{2,1,0:T(8,128)(2,1)S(1)}, bf16[4,128,256]{2,1,0:T(8,128)(2,1)S(1)}, u32[]{:S(2)}, u32[]{:S(2)}) collective-permute-start(bf16[4,128,256]{2,1,0:T(8,128)(2,1)S(1)} %all-to-all-done.own), channel_id=1, source_target_pairs={{0,4},{4,8},{8,12},{12,16},{16,20},{20,24},{24,28},{28,32},{32,36}... | collective-permute-start | bytes 786440 | tf_op jit(solution)/shard_map/ppermute | solution.py:132
  50.8 13.1 %collective-permute-start.3 = (bf16[4,128,256]{2,1,0:T(8,128)(2,1)S(1)}, bf16[4,128,256]{2,1,0:T(8,128)(2,1)S(1)}, u32[]{:S(2)}, u32[]{:S(2)}) collective-permute-start(bf16[4,128,256]{2,1,0:T(8,128)(2,1)S(1)} %all-to-all-done.own), channel_id=1, source_target_pairs={{0,60},{4,0},{8,4},{12,8},{16,12},{20,16},{24,20},{28,24},{32,28},... | collective-permute-start | bytes 786440 | tf_op jit(solution)/shard_map/ppermute | solution.py:132
  55.6 12.7 %copy-start.1 = (bf16[1,1,32,128,128]{4,3,2,1,0:T(8,128)(2,1)S(1)}, bf16[1,1,32,128,128]{4,3,2,1,0:T(8,128)(2,1)}, u32[]{:S(2)}) copy-start(bf16[1,1,32,128,128]{4,3,2,1,0:T(8,128)(2,1)} %param.6) | copy-start | bytes 3145732
  55.6 27.8 %all-to-all-start.1 = ((bf16[4,128,256]{2,1,0:T(8,128)(2,1)}), bf16[4,128,256]{2,1,0:T(8,128)(2,1)S(1)}, u32[]{:S(2)}, u32[]{:S(2)}) async-start(bf16[4,128,256]{2,1,0:T(8,128)(2,1)} %add_convert_fusion), calls=%async_computation.1 | async-start | bytes 524288 | tf_op jit(solution)/shard_map/all_to_all | solution.py:187
  65.1 12.4 %collective-permute-start.7 = (bf16[2,8,128,128]{3,2,1,0:T(8,128)(2,1)S(1)}, bf16[2,8,128,128]{3,2,1,0:T(8,128)(2,1)S(1)}, u32[]{:S(2)}, u32[]{:S(2)}) collective-permute-start(bf16[2,8,128,128]{3,2,1,0:T(8,128)(2,1)S(1)} %get-tuple-element.33), channel_id=1, source_target_pairs={{0,1},{1,0},{2,3},{3,2},{4,5},{5,4},{6,7},{7,6},{8,9},{9,8},{10,11... | collective-permute-start | bytes 1572872 | tf_op jit(solution)/shard_map/ppermute | solution.py:146
  69.5 7.3 %collective-permute-start.6 = (bf16[4,128,128]{2,1,0:T(8,128)(2,1)S(1)}, bf16[4,128,128]{2,1,0:T(8,128)(2,1)S(1)}, u32[]{:S(2)}, u32[]{:S(2)}) collective-permute-start(bf16[4,128,128]{2,1,0:T(8,128)(2,1)S(1)} %get-tuple-element.25), channel_id=1, source_target_pairs={{0,64},{64,0},{128,192},{192,128},{256,320},{320,256},{384,448},{4... | collective-permute-start | bytes 393224 | tf_op jit(solution)/shard_map/ppermute | solution.py:146
  77.5 10.8 %collective-permute-start.8 = (bf16[8,128,128]{2,1,0:T(8,128)(2,1)S(1)}, bf16[8,128,128]{2,1,0:T(8,128)(2,1)S(1)}, u32[]{:S(2)}, u32[]{:S(2)}) collective-permute-start(bf16[8,128,128]{2,1,0:T(8,128)(2,1)S(1)} %fusion), channel_id=1, source_target_pairs={{0,2},{1,3},{2,0},{3,1},{4,6},{5,7},{6,4},{7,5},{8,10},{9,11},{10,... | collective-permute-start | bytes 786440 | tf_op jit(solution)/shard_map/ppermute | solution.py:146
  84.0 10.3 %all-to-all-start.2 = ((bf16[4,128,128]{2,1,0:T(8,128)(2,1)}), bf16[4,128,128]{2,1,0:T(8,128)(2,1)S(1)}, u32[]{:S(2)}, u32[]{:S(2)}) async-start(bf16[4,128,128]{2,1,0:T(8,128)(2,1)} %add_convert_fusion.1), calls=%async_computation.2 | async-start | bytes 262144 | tf_op jit(solution)/shard_map/all_to_all | solution.py:214

commit v5 on v4

--- a/solution.py
+++ b/solution.py
@@ -177,13 +177,13 @@
         2 * capacity * token_count * block * block,
         *info, tokens, weights,
     )
+    from_far = both_ways(far, 2)
     from_below = shifted(up, "col", 1)
     from_above = shifted(down, "col", -1)
-    from_far = both_ways(far, 2)
-    grads_own, from_below, from_above, from_far = lax.optimization_barrier(
-        (grads_own, from_below, from_above, from_far)
-    )
-    hidden_near = summed(own, from_below, from_above, from_far)
+    grads_own, from_far, from_below, from_above = lax.optimization_barrier(
+        (grads_own, from_far, from_below, from_above)
+    )
+    hidden_near = summed(own, from_far, from_below, from_above)
     hidden_parts = lax.all_to_all(hidden_near, "col", 0, 0, tiled=True, axis_index_groups=strided)
     above = shifted(grads_own, "col", -1)
     below = shifted(grads_own, "col", 1)

time: 95.7 us -> 94.7 us (0.990)
  starting transfers between devices: 58 us -> 55.8 us
    ppermute x2, waiting for transfers between devices: 3.8 us -> 8.15 us  [both_ways(): return lax.ppermute(x, ('col', 'dp'), pairs)]
    ppermute x4, starting transfers between devices: 17.5 us -> 14.1 us  [shifted(): return lax.ppermute(x, axis, [(i, (i + by) % n) for i in range(n)])]
    ppermute x4, waiting for transfers between devices: 7.89 us -> 4.57 us  [shifted(): return lax.ppermute(x, axis, [(i, (i + by) % n) for i in range(n)])]
    ppermute x3, waiting for transfers between devices: 4.65 us -> 6.82 us  [swapped(): lax.ppermute(x, axis, [(i, i ^ bit) for i in range(lax.axis_size(axis))])]
    all_to_all x1, waiting for transfers between devices: 5.16 us -> 3.48 us  [local(): lax.all_to_all(features, 'row', 0, 0, tiled=True, axis_index_groups=along_x)]
    ppermute x2, starting transfers between devices: 3.83 us -> 5.41 us  [both_ways(): return lax.ppermute(x, ('col', 'dp'), pairs)]
    ppermute x3, starting transfers between devices: 8.92 us -> 7.71 us  [swapped(): lax.ppermute(x, axis, [(i, i ^ bit) for i in range(lax.axis_size(axis))])]
    all_to_all x1, waiting for transfers between devices: 2.68 us -> 1.53 us  [local(): lax.all_to_all(hidden_near, 'col', 0, 0, tiled=True, axis_index_groups=st...]
where the time goes in v5:
time: 94.7 us; the launch traced here: 93 us
  starting transfers between devices  55.8 us (59%)
  waiting for transfers between devices  24.6 us (26%)
  Pallas kernels  4.73 us (5%)
  local copies, waits for them, and re-layouts  3.47 us (4%)
  other arithmetic  3.11 us (3%)
  between operations  1.41 us (1%)
    all_to_all x1, starting transfers between devices, local(): lax.all_to_all(copies, 'col', 0, 0, tiled=True, axis_index_groups=strided)  15.2 us
    ppermute x4, starting transfers between devices, shifted(): return lax.ppermute(x, axis, [(i, (i + by) % n) for i in range(n)])  14.1 us
    all_to_all x1, starting transfers between devices, local(): lax.all_to_all(hidden_near, 'col', 0, 0, tiled=True, axis_index_groups=st...  9.03 us
    ppermute x2, waiting for transfers between devices, both_ways(): return lax.ppermute(x, ('col', 'dp'), pairs)  8.15 us
    ppermute x3, starting transfers between devices, swapped(): lax.ppermute(x, axis, [(i, i ^ bit) for i in range(lax.axis_size(axis))])  7.71 us
    ppermute x3, waiting for transfers between devices, swapped(): lax.ppermute(x, axis, [(i, i ^ bit) for i in range(lax.axis_size(axis))])  6.82 us
    ppermute x2, starting transfers between devices, both_ways(): return lax.ppermute(x, ('col', 'dp'), pairs)  5.41 us
    ppermute x4, waiting for transfers between devices, shifted(): return lax.ppermute(x, axis, [(i, (i + by) % n) for i in range(n)])  4.57 us
  transfers between devices with their start and end apart: 12, of which 6 were waited for; matrix products, arithmetic and copies ran while one was open for 3% of the time, Pallas kernels for 5%

profile of v5, /device:TPU:24, one launch (start us, length us, event | category | flops | bytes accessed | tf_op | source)
XLA Modules:
  0.0 93.0 jit_solution(9126134073352153624)
XLA Ops:
  0.6 1.6 %broadcast_in_dim.13 = bf16[4,128,256]{2,1,0:T(8,128)(2,1)} broadcast(bf16[128,256]{1,0:T(8,128)(2,1)} %param.9), dimensions={1,2} | broadcast | bytes 327680 | tf_op jit(solution)/shard_map/broadcast_in_dim | solution.py:171
  2.2 15.2 %all-to-all-start = ((bf16[4,128,256]{2,1,0:T(8,128)(2,1)}), bf16[4,128,256]{2,1,0:T(8,128)(2,1)S(1)}, u32[]{:S(2)}, u32[]{:S(2)}) async-start(bf16[4,128,256]{2,1,0:T(8,128)(2,1)} %broadcast_in_dim.13), calls=%async_computation | async-start | bytes 524288 | tf_op jit(solution)/shard_map/all_to_all | solution.py:172
  18.1 0.1 add_bitcast_fusion.dp_place
  18.1 0.7 copy-done.3
  18.8 1.2 %copy-done = bf16[1,1,32,128,128]{4,3,2,1,0:T(8,128)(2,1)S(1)} copy-done((bf16[1,1,32,128,128]{4,3,2,1,0:T(8,128)(2,1)S(1)}, bf16[1,1,32,128,128]{4,3,2,1,0:T(8,128)(2,1)}, u32[]{:S(2)}) %copy-start) | copy-done | bytes 1048600
  20.0 1.6 %shard_map.76 = (bf16[4,128,256]{2,1,0:T(8,128)(2,1)S(1)}, bf16[4,128,256]{2,1,0:T(8,128)(2,1)S(1)}, bf16[4,128,256]{2,1,0:T(8,128)(2,1)S(1)}, bf16[4,128,256]{2,1,0:T(8,128)(2,1)S(1)}) custom-call(s32[2,32]{1,0:T(2,128)S(1)} %bitcast.22, s32[1,1]{1,0:T(1,128)S(6)} %copy.8.live_count, s32[1,1]{1,0:T(1,128)} %bitcast.1.plane, ...), custom_call_target="tpu_custom_call" | custom-call | flops 134217728 | bytes 524288 | tf_op jit(solution)/shard_map/pallas_call | solution.py:100
  21.6 3.4 %collective-permute-start = (bf16[4,128,256]{2,1,0:T(8,128)(2,1)S(1)}, bf16[4,128,256]{2,1,0:T(8,128)(2,1)S(1)}, u32[]{:S(2)}, u32[]{:S(2)}) collective-permute-start(bf16[4,128,256]{2,1,0:T(8,128)(2,1)S(1)} %get-tuple-element.20), channel_id=1, source_target_pairs={{0,8},{1,57},{2,10},{3,59},{4,12},{5,61},{6,14},{7,63},{8,16},{9,1... | collective-permute-start | bytes 786440 | tf_op jit(solution)/shard_map/ppermute | solution.py:142
  25.0 2.9 %collective-permute-start.1 = (bf16[4,128,256]{2,1,0:T(8,128)(2,1)S(1)}, bf16[4,128,256]{2,1,0:T(8,128)(2,1)S(1)}, u32[]{:S(2)}, u32[]{:S(2)}) collective-permute-start(bf16[4,128,256]{2,1,0:T(8,128)(2,1)S(1)} %get-tuple-element.21), channel_id=1, source_target_pairs={{0,4},{4,8},{8,12},{12,16},{16,20},{20,24},{24,28},{28,32},{32,36}... | collective-permute-start | bytes 786440 | tf_op jit(solution)/shard_map/ppermute | solution.py:132
  28.0 4.1 %collective-permute-start.2 = (bf16[4,128,256]{2,1,0:T(8,128)(2,1)S(1)}, bf16[4,128,256]{2,1,0:T(8,128)(2,1)S(1)}, u32[]{:S(2)}, u32[]{:S(2)}) collective-permute-start(bf16[4,128,256]{2,1,0:T(8,128)(2,1)S(1)} %get-tuple-element.22), channel_id=1, source_target_pairs={{0,60},{4,0},{8,4},{12,8},{16,12},{20,16},{24,20},{28,24},{32,28},... | collective-permute-start | bytes 786440 | tf_op jit(solution)/shard_map/ppermute | solution.py:132
  32.1 8.2 %collective-permute-done = bf16[4,128,256]{2,1,0:T(8,128)(2,1)S(1)} collective-permute-done((bf16[4,128,256]{2,1,0:T(8,128)(2,1)S(1)}, bf16[4,128,256]{2,1,0:T(8,128)(2,1)S(1)}, u32[]{:S(2)}, u32[]{:S(2)}) %collective-permute-start) | collective-permute-done | bytes 262176 | tf_op jit(solution)/shard_map/ppermute | solution.py:142
  40.2 4.6 %collective-permute-done.1 = bf16[4,128,256]{2,1,0:T(8,128)(2,1)S(1)} collective-permute-done((bf16[4,128,256]{2,1,0:T(8,128)(2,1)S(1)}, bf16[4,128,256]{2,1,0:T(8,128)(2,1)S(1)}, u32[]{:S(2)}, u32[]{:S(2)}) %collective-permute-start.1) | collective-permute-done | bytes 262176 | tf_op jit(solution)/shard_map/ppermute | solution.py:132
  44.8 0.0 all-to-all-done.own
  44.8 2.0 %collective-permute-start.5 = (bf16[4,128,256]{2,1,0:T(8,128)(2,1)S(1)}, bf16[4,128,256]{2,1,0:T(8,128)(2,1)S(1)}, u32[]{:S(2)}, u32[]{:S(2)}) collective-permute-start(bf16[4,128,256]{2,1,0:T(8,128)(2,1)S(1)} %all-to-all-done.own), channel_id=1, source_target_pairs={{0,8},{1,57},{2,10},{3,59},{4,12},{5,61},{6,14},{7,63},{8,16},{9,1... | collective-permute-start | bytes 786440 | tf_op jit(solution)/shard_map/ppermute | solution.py:142
  46.8 3.6 %collective-permute-start.4 = (bf16[4,128,256]{2,1,0:T(8,128)(2,1)S(1)}, bf16[4,128,256]{2,1,0:T(8,128)(2,1)S(1)}, u32[]{:S(2)}, u32[]{:S(2)}) collective-permute-start(bf16[4,128,256]{2,1,0:T(8,128)(2,1)S(1)} %all-to-all-done.own), channel_id=1, source_target_pairs={{0,4},{4,8},{8,12},{12,16},{16,20},{20,24},{24,28},{28,32},{32,36}... | collective-permute-start | bytes 786440 | tf_op jit(solution)/shard_map/ppermute | solution.py:132
  50.5 3.4 %collective-permute-start.3 = (bf16[4,128,256]{2,1,0:T(8,128)(2,1)S(1)}, bf16[4,128,256]{2,1,0:T(8,128)(2,1)S(1)}, u32[]{:S(2)}, u32[]{:S(2)}) collective-permute-start(bf16[4,128,256]{2,1,0:T(8,128)(2,1)S(1)} %all-to-all-done.own), channel_id=1, source_target_pairs={{0,60},{4,0},{8,4},{12,8},{16,12},{20,16},{24,20},{28,24},{32,28},... | collective-permute-start | bytes 786440 | tf_op jit(solution)/shard_map/ppermute | solution.py:132
  53.9 0.8 add_convert_fusion
  54.8 9.0 %all-to-all-start.1 = ((bf16[4,128,256]{2,1,0:T(8,128)(2,1)}), bf16[4,128,256]{2,1,0:T(8,128)(2,1)S(1)}, u32[]{:S(2)}, u32[]{:S(2)}) async-start(bf16[4,128,256]{2,1,0:T(8,128)(2,1)} %add_convert_fusion), calls=%async_computation.1 | async-start | bytes 524288 | tf_op jit(solution)/shard_map/all_to_all | solution.py:187
  63.8 1.2 %shard_map.79 = (bf16[8,128,128]{2,1,0:T(8,128)(2,1)S(1)}, bf16[8,128,128]{2,1,0:T(8,128)(2,1)S(1)}, bf16[2,8,128,128]{3,2,1,0:T(8,128)(2,1)S(1)}) custom-call(s32[2,32]{1,0:T(2,128)S(1)} %bitcast.23, s32[1,1]{1,0:T(1,128)S(6)} %copy.8.live_count, s32[1,1]{1,0:T(1,128)} %bitcast.1.plane, s32[1,2]{1,0:T(1,128)S(1)} %add_bitcast_fusion.dp_place, ...), custom_call_target="tpu_custom_call" | custom-call | flops 1000 | bytes 3 | tf_op jit(solution)/shard_map/pallas_call | solution.py:100
  65.1 1.9 %collective-permute-start.7 = (bf16[2,8,128,128]{3,2,1,0:T(8,128)(2,1)S(1)}, bf16[2,8,128,128]{3,2,1,0:T(8,128)(2,1)S(1)}, u32[]{:S(2)}, u32[]{:S(2)}) collective-permute-start(bf16[2,8,128,128]{3,2,1,0:T(8,128)(2,1)S(1)} %get-tuple-element.33), channel_id=1, source_target_pairs={{0,1},{1,0},{2,3},{3,2},{4,5},{5,4},{6,7},{7,6},{8,9},{9,8},{10,11... | collective-permute-start | bytes 1572872 | tf_op jit(solution)/shard_map/ppermute | solution.py:146
  67.0 1.2 %shard_map.77 = (bf16[4,128,128]{2,1,0:T(8,128)(2,1)S(1)}, bf16[4,128,128]{2,1,0:T(8,128)(2,1)S(1)}) custom-call(s32[2,32]{1,0:T(2,128)S(1)} %bitcast.24, s32[1,1]{1,0:T(1,128)S(6)} %copy.8.live_count, s32[1,1]{1,0:T(1,128)} %bitcast.1.plane, s32[1,2]{1,0:T(1,128)S(1)} %add_bitcast_fusion.dp_place, bf16[128,1024]{1,0:T(8,128)(2,1)S(1)} %copy-done.2, ...), custom_call_target="tpu_custom_call" | custom-call | flops 1000 | bytes 3 | tf_op jit(solution)/shard_map/pallas_call | solution.py:100
  68.2 2.7 %collective-permute-start.6 = (bf16[4,128,128]{2,1,0:T(8,128)(2,1)S(1)}, bf16[4,128,128]{2,1,0:T(8,128)(2,1)S(1)}, u32[]{:S(2)}, u32[]{:S(2)}) collective-permute-start(bf16[4,128,128]{2,1,0:T(8,128)(2,1)S(1)} %get-tuple-element.25), channel_id=1, source_target_pairs={{0,64},{64,0},{128,192},{192,128},{256,320},{320,256},{384,448},{4... | collective-permute-start | bytes 393224 | tf_op jit(solution)/shard_map/ppermute | solution.py:146
  70.9 5.1 %collective-permute-done.6 = bf16[4,128,128]{2,1,0:T(8,128)(2,1)S(1)} collective-permute-done((bf16[4,128,128]{2,1,0:T(8,128)(2,1)S(1)}, bf16[4,128,128]{2,1,0:T(8,128)(2,1)S(1)}, u32[]{:S(2)}, u32[]{:S(2)}) %collective-permute-start.6) | collective-permute-done | bytes 131104 | tf_op jit(solution)/shard_map/ppermute | solution.py:146
  76.0 0.7 add_convert_fusion.1
  76.7 0.1 fusion
  76.8 3.1 %collective-permute-start.8 = (bf16[8,128,128]{2,1,0:T(8,128)(2,1)S(1)}, bf16[8,128,128]{2,1,0:T(8,128)(2,1)S(1)}, u32[]{:S(2)}, u32[]{:S(2)}) collective-permute-start(bf16[8,128,128]{2,1,0:T(8,128)(2,1)S(1)} %fusion), channel_id=1, source_target_pairs={{0,2},{1,3},{2,0},{3,1},{4,6},{5,7},{6,4},{7,5},{8,10},{9,11},{10,... | collective-permute-start | bytes 786440 | tf_op jit(solution)/shard_map/ppermute | solution.py:146
  79.9 1.5 %all-to-all-done.1.parts = bf16[4,128,256]{2,1,0:T(8,128)(2,1)S(1)} async-done(((bf16[4,128,256]{2,1,0:T(8,128)(2,1)}), bf16[4,128,256]{2,1,0:T(8,128)(2,1)S(1)}, u32[]{:S(2)}, u32[]{:S(2)}) %all-to-all-start.1) | async-done | bytes 262176 | tf_op jit(solution)/shard_map/all_to_all | solution.py:187
  81.5 0.7 shard_map.78
  82.1 4.3 %all-to-all-start.2 = ((bf16[4,128,128]{2,1,0:T(8,128)(2,1)}), bf16[4,128,128]{2,1,0:T(8,128)(2,1)S(1)}, u32[]{:S(2)}, u32[]{:S(2)}) async-start(bf16[4,128,128]{2,1,0:T(8,128)(2,1)} %add_convert_fusion.1), calls=%async_computation.2 | async-start | bytes 262144 | tf_op jit(solution)/shard_map/all_to_all | solution.py:214
  86.4 1.7 %collective-permute-done.8 = bf16[8,128,128]{2,1,0:T(8,128)(2,1)S(1)} collective-permute-done((bf16[8,128,128]{2,1,0:T(8,128)(2,1)S(1)}, bf16[8,128,128]{2,1,0:T(8,128)(2,1)S(1)}, u32[]{:S(2)}, u32[]{:S(2)}) %collective-permute-start.8) | collective-permute-done | bytes 262176 | tf_op jit(solution)/shard_map/ppermute | solution.py:146
  88.1 0.8 fusion.2
  88.9 3.5 %all-to-all-done.2 = bf16[4,128,128]{2,1,0:T(8,128)(2,1)S(1)} async-done(((bf16[4,128,128]{2,1,0:T(8,128)(2,1)}), bf16[4,128,128]{2,1,0:T(8,128)(2,1)S(1)}, u32[]{:S(2)}, u32[]{:S(2)}) %all-to-all-start.2) | async-done | bytes 131104 | tf_op jit(solution)/shard_map/all_to_all | solution.py:214
  92.4 0.6 fusion.3
  (11 shorter events, 0.0 us)
Async XLA Ops:
  2.2 15.9 %copy-start.2 = (bf16[128,1024]{1,0:T(8,128)(2,1)S(1)}, bf16[128,1024]{1,0:T(8,128)(2,1)}, u32[]{:S(2)}) copy-start(bf16[128,1024]{1,0:T(8,128)(2,1)} %tokens.5) | copy-start | bytes 786436
  2.2 42.6 %all-to-all-start = ((bf16[4,128,256]{2,1,0:T(8,128)(2,1)}), bf16[4,128,256]{2,1,0:T(8,128)(2,1)S(1)}, u32[]{:S(2)}, u32[]{:S(2)}) async-start(bf16[4,128,256]{2,1,0:T(8,128)(2,1)} %broadcast_in_dim.13), calls=%async_computation | async-start | bytes 524288 | tf_op jit(solution)/shard_map/all_to_all | solution.py:172
  18.1 0.7 copy-start.3
  18.8 1.2 %copy-start = (bf16[1,1,32,128,128]{4,3,2,1,0:T(8,128)(2,1)S(1)}, bf16[1,1,32,128,128]{4,3,2,1,0:T(8,128)(2,1)}, u32[]{:S(2)}) copy-start(bf16[1,1,32,128,128]{4,3,2,1,0:T(8,128)(2,1)} %param.6) | copy-start | bytes 3145732
  21.6 18.6 %collective-permute-start = (bf16[4,128,256]{2,1,0:T(8,128)(2,1)S(1)}, bf16[4,128,256]{2,1,0:T(8,128)(2,1)S(1)}, u32[]{:S(2)}, u32[]{:S(2)}) collective-permute-start(bf16[4,128,256]{2,1,0:T(8,128)(2,1)S(1)} %get-tuple-element.20), channel_id=1, source_target_pairs={{0,8},{1,57},{2,10},{3,59},{4,12},{5,61},{6,14},{7,63},{8,16},{9,1... | collective-permute-start | bytes 786440 | tf_op jit(solution)/shard_map/ppermute | solution.py:142
  25.0 19.8 %collective-permute-start.1 = (bf16[4,128,256]{2,1,0:T(8,128)(2,1)S(1)}, bf16[4,128,256]{2,1,0:T(8,128)(2,1)S(1)}, u32[]{:S(2)}, u32[]{:S(2)}) collective-permute-start(bf16[4,128,256]{2,1,0:T(8,128)(2,1)S(1)} %get-tuple-element.21), channel_id=1, source_target_pairs={{0,4},{4,8},{8,12},{12,16},{16,20},{20,24},{24,28},{28,32},{32,36}... | collective-permute-start | bytes 786440 | tf_op jit(solution)/shard_map/ppermute | solution.py:132
  28.0 16.9 %collective-permute-start.2 = (bf16[4,128,256]{2,1,0:T(8,128)(2,1)S(1)}, bf16[4,128,256]{2,1,0:T(8,128)(2,1)S(1)}, u32[]{:S(2)}, u32[]{:S(2)}) collective-permute-start(bf16[4,128,256]{2,1,0:T(8,128)(2,1)S(1)} %get-tuple-element.22), channel_id=1, source_target_pairs={{0,60},{4,0},{8,4},{12,8},{16,12},{20,16},{24,20},{28,24},{32,28},... | collective-permute-start | bytes 786440 | tf_op jit(solution)/shard_map/ppermute | solution.py:132
  44.8 19.0 %collective-permute-start.5 = (bf16[4,128,256]{2,1,0:T(8,128)(2,1)S(1)}, bf16[4,128,256]{2,1,0:T(8,128)(2,1)S(1)}, u32[]{:S(2)}, u32[]{:S(2)}) collective-permute-start(bf16[4,128,256]{2,1,0:T(8,128)(2,1)S(1)} %all-to-all-done.own), channel_id=1, source_target_pairs={{0,8},{1,57},{2,10},{3,59},{4,12},{5,61},{6,14},{7,63},{8,16},{9,1... | collective-permute-start | bytes 786440 | tf_op jit(solution)/shard_map/ppermute | solution.py:142
  46.8 16.9 %collective-permute-start.4 = (bf16[4,128,256]{2,1,0:T(8,128)(2,1)S(1)}, bf16[4,128,256]{2,1,0:T(8,128)(2,1)S(1)}, u32[]{:S(2)}, u32[]{:S(2)}) collective-permute-start(bf16[4,128,256]{2,1,0:T(8,128)(2,1)S(1)} %all-to-all-done.own), channel_id=1, source_target_pairs={{0,4},{4,8},{8,12},{12,16},{16,20},{20,24},{24,28},{28,32},{32,36}... | collective-permute-start | bytes 786440 | tf_op jit(solution)/shard_map/ppermute | solution.py:132
  50.5 13.3 %collective-permute-start.3 = (bf16[4,128,256]{2,1,0:T(8,128)(2,1)S(1)}, bf16[4,128,256]{2,1,0:T(8,128)(2,1)S(1)}, u32[]{:S(2)}, u32[]{:S(2)}) collective-permute-start(bf16[4,128,256]{2,1,0:T(8,128)(2,1)S(1)} %all-to-all-done.own), channel_id=1, source_target_pairs={{0,60},{4,0},{8,4},{12,8},{16,12},{20,16},{24,20},{28,24},{32,28},... | collective-permute-start | bytes 786440 | tf_op jit(solution)/shard_map/ppermute | solution.py:132
  54.8 12.2 %copy-start.1 = (bf16[1,1,32,128,128]{4,3,2,1,0:T(8,128)(2,1)S(1)}, bf16[1,1,32,128,128]{4,3,2,1,0:T(8,128)(2,1)}, u32[]{:S(2)}) copy-start(bf16[1,1,32,128,128]{4,3,2,1,0:T(8,128)(2,1)} %param.6) | copy-start | bytes 3145732
  54.8 26.7 %all-to-all-start.1 = ((bf16[4,128,256]{2,1,0:T(8,128)(2,1)}), bf16[4,128,256]{2,1,0:T(8,128)(2,1)S(1)}, u32[]{:S(2)}, u32[]{:S(2)}) async-start(bf16[4,128,256]{2,1,0:T(8,128)(2,1)} %add_convert_fusion), calls=%async_computation.1 | async-start | bytes 524288 | tf_op jit(solution)/shard_map/all_to_all | solution.py:187
  65.1 11.7 %collective-permute-start.7 = (bf16[2,8,128,128]{3,2,1,0:T(8,128)(2,1)S(1)}, bf16[2,8,128,128]{3,2,1,0:T(8,128)(2,1)S(1)}, u32[]{:S(2)}, u32[]{:S(2)}) collective-permute-start(bf16[2,8,128,128]{3,2,1,0:T(8,128)(2,1)S(1)} %get-tuple-element.33), channel_id=1, source_target_pairs={{0,1},{1,0},{2,3},{3,2},{4,5},{5,4},{6,7},{7,6},{8,9},{9,8},{10,11... | collective-permute-start | bytes 1572872 | tf_op jit(solution)/shard_map/ppermute | solution.py:146
  68.2 7.8 %collective-permute-start.6 = (bf16[4,128,128]{2,1,0:T(8,128)(2,1)S(1)}, bf16[4,128,128]{2,1,0:T(8,128)(2,1)S(1)}, u32[]{:S(2)}, u32[]{:S(2)}) collective-permute-start(bf16[4,128,128]{2,1,0:T(8,128)(2,1)S(1)} %get-tuple-element.25), channel_id=1, source_target_pairs={{0,64},{64,0},{128,192},{192,128},{256,320},{320,256},{384,448},{4... | collective-permute-start | bytes 393224 | tf_op jit(solution)/shard_map/ppermute | solution.py:146
  76.8 11.3 %collective-permute-start.8 = (bf16[8,128,128]{2,1,0:T(8,128)(2,1)S(1)}, bf16[8,128,128]{2,1,0:T(8,128)(2,1)S(1)}, u32[]{:S(2)}, u32[]{:S(2)}) collective-permute-start(bf16[8,128,128]{2,1,0:T(8,128)(2,1)S(1)} %fusion), channel_id=1, source_target_pairs={{0,2},{1,3},{2,0},{3,1},{4,6},{5,7},{6,4},{7,5},{8,10},{9,11},{10,... | collective-permute-start | bytes 786440 | tf_op jit(solution)/shard_map/ppermute | solution.py:146
  82.1 10.3 %all-to-all-start.2 = ((bf16[4,128,128]{2,1,0:T(8,128)(2,1)}), bf16[4,128,128]{2,1,0:T(8,128)(2,1)S(1)}, u32[]{:S(2)}, u32[]{:S(2)}) async-start(bf16[4,128,128]{2,1,0:T(8,128)(2,1)} %add_convert_fusion.1), calls=%async_computation.2 | async-start | bytes 262144 | tf_op jit(solution)/shard_map/all_to_all | solution.py:214

commit v6 on v5

--- a/solution.py
+++ b/solution.py
@@ -199,7 +199,6 @@
     )
     received = swapped(send, "dp", 1)
     theirs = summed(keep_far, received[0])
-    from_side = swapped(theirs, "dp", 2)
     kept, sent = call(
         features_kernel,
         [(col_blocks // 2, *blocks)] * 2,
@@ -207,6 +206,8 @@
         low_cost,
         *info, tokens, weights, grads_own, above, below, across,
     )
+    sent, theirs = lax.optimization_barrier((sent, theirs))
+    from_side = swapped(theirs, "dp", 2)
     features = summed(kept, swapped(sent, "row", 1))
     hidden = call_sum(hidden_parts, high_cost)
     features, hidden = lax.optimization_barrier((features, hidden))

time: 94.7 us -> 95.4 us (level)
    ppermute x3, waiting for transfers between devices: 6.82 us -> 0.63 us  [swapped(): lax.ppermute(x, axis, [(i, i ^ bit) for i in range(lax.axis_size(axis))])]
    all_to_all x1, waiting for transfers between devices: 1.53 us -> 7.01 us  [local(): lax.all_to_all(hidden_near, 'col', 0, 0, tiled=True, axis_index_groups=st...]
    all_to_all x1, waiting for transfers between devices: 3.48 us -> 5.16 us  [local(): lax.all_to_all(features, 'row', 0, 0, tiled=True, axis_index_groups=along_x)]
    unnamed x8 -> x12, local copies, waits for them, and re-layouts: 1.91 us -> 1.92 us
  transfers between devices with their start and end apart: 12 -> 12, of which waited for: 6 -> 5; matrix products, arithmetic and copies ran while one was open for 3% -> 3% of each run, Pallas kernels for 5% -> 5%
where the time goes in v6:
time: 95.4 us; the launch traced here: 93.7 us
  starting transfers between devices  55.5 us (58%)
  waiting for transfers between devices  25.5 us (27%)
  Pallas kernels  4.73 us (5%)
  local copies, waits for them, and re-layouts  3.47 us (4%)
  other arithmetic  3.13 us (3%)
  between operations  1.42 us (1%)
    all_to_all x1, starting transfers between devices, local(): lax.all_to_all(copies, 'col', 0, 0, tiled=True, axis_index_groups=strided)  15.2 us
    ppermute x4, starting transfers between devices, shifted(): return lax.ppermute(x, axis, [(i, (i + by) % n) for i in range(n)])  14.1 us
    all_to_all x1, starting transfers between devices, local(): lax.all_to_all(hidden_near, 'col', 0, 0, tiled=True, axis_index_groups=st...  9.03 us
    ppermute x2, waiting for transfers between devices, both_ways(): return lax.ppermute(x, ('col', 'dp'), pairs)  8.16 us
    ppermute x3, starting transfers between devices, swapped(): lax.ppermute(x, axis, [(i, i ^ bit) for i in range(lax.axis_size(axis))])  7.41 us
    all_to_all x1, waiting for transfers between devices, local(): lax.all_to_all(hidden_near, 'col', 0, 0, tiled=True, axis_index_groups=st...  7.01 us
    ppermute x2, starting transfers between devices, both_ways(): return lax.ppermute(x, ('col', 'dp'), pairs)  5.41 us
    all_to_all x1, waiting for transfers between devices, local(): lax.all_to_all(features, 'row', 0, 0, tiled=True, axis_index_groups=along_x)  5.16 us
  transfers between devices with their start and end apart: 12, of which 5 were waited for; matrix products, arithmetic and copies ran while one was open for 3% of the time, Pallas kernels for 5%

profile of v6, /device:TPU:24, one launch (start us, length us, event | category | flops | bytes accessed | tf_op | source)
XLA Modules:
  0.0 93.7 jit_solution(18094590188710836716)
XLA Ops:
  0.6 1.6 %broadcast_in_dim.13 = bf16[4,128,256]{2,1,0:T(8,128)(2,1)} broadcast(bf16[128,256]{1,0:T(8,128)(2,1)} %param.9), dimensions={1,2} | broadcast | bytes 327680 | tf_op jit(solution)/shard_map/broadcast_in_dim | solution.py:171
  2.2 15.2 %all-to-all-start = ((bf16[4,128,256]{2,1,0:T(8,128)(2,1)}), bf16[4,128,256]{2,1,0:T(8,128)(2,1)S(1)}, u32[]{:S(2)}, u32[]{:S(2)}) async-start(bf16[4,128,256]{2,1,0:T(8,128)(2,1)} %broadcast_in_dim.13), calls=%async_computation | async-start | bytes 524288 | tf_op jit(solution)/shard_map/all_to_all | solution.py:172
  18.1 0.1 add_bitcast_fusion.dp_place
  18.1 0.7 copy-done.3
  18.8 1.2 %copy-done = bf16[1,1,32,128,128]{4,3,2,1,0:T(8,128)(2,1)S(1)} copy-done((bf16[1,1,32,128,128]{4,3,2,1,0:T(8,128)(2,1)S(1)}, bf16[1,1,32,128,128]{4,3,2,1,0:T(8,128)(2,1)}, u32[]{:S(2)}) %copy-start) | copy-done | bytes 1048600
  20.0 1.6 %shard_map.76 = (bf16[4,128,256]{2,1,0:T(8,128)(2,1)S(1)}, bf16[4,128,256]{2,1,0:T(8,128)(2,1)S(1)}, bf16[4,128,256]{2,1,0:T(8,128)(2,1)S(1)}, bf16[4,128,256]{2,1,0:T(8,128)(2,1)S(1)}) custom-call(s32[2,32]{1,0:T(2,128)S(1)} %bitcast.22, s32[1,1]{1,0:T(1,128)S(6)} %copy.8.live_count, s32[1,1]{1,0:T(1,128)} %bitcast.1.plane, ...), custom_call_target="tpu_custom_call" | custom-call | flops 134217728 | bytes 524288 | tf_op jit(solution)/shard_map/pallas_call | solution.py:100
  21.6 3.4 %collective-permute-start = (bf16[4,128,256]{2,1,0:T(8,128)(2,1)S(1)}, bf16[4,128,256]{2,1,0:T(8,128)(2,1)S(1)}, u32[]{:S(2)}, u32[]{:S(2)}) collective-permute-start(bf16[4,128,256]{2,1,0:T(8,128)(2,1)S(1)} %get-tuple-element.22), channel_id=1, source_target_pairs={{0,8},{1,57},{2,10},{3,59},{4,12},{5,61},{6,14},{7,63},{8,16},{9,1... | collective-permute-start | bytes 786440 | tf_op jit(solution)/shard_map/ppermute | solution.py:142
  25.0 2.9 %collective-permute-start.1 = (bf16[4,128,256]{2,1,0:T(8,128)(2,1)S(1)}, bf16[4,128,256]{2,1,0:T(8,128)(2,1)S(1)}, u32[]{:S(2)}, u32[]{:S(2)}) collective-permute-start(bf16[4,128,256]{2,1,0:T(8,128)(2,1)S(1)} %get-tuple-element.23), channel_id=1, source_target_pairs={{0,4},{4,8},{8,12},{12,16},{16,20},{20,24},{24,28},{28,32},{32,36}... | collective-permute-start | bytes 786440 | tf_op jit(solution)/shard_map/ppermute | solution.py:132
  28.0 4.1 %collective-permute-start.2 = (bf16[4,128,256]{2,1,0:T(8,128)(2,1)S(1)}, bf16[4,128,256]{2,1,0:T(8,128)(2,1)S(1)}, u32[]{:S(2)}, u32[]{:S(2)}) collective-permute-start(bf16[4,128,256]{2,1,0:T(8,128)(2,1)S(1)} %get-tuple-element.24), channel_id=1, source_target_pairs={{0,60},{4,0},{8,4},{12,8},{16,12},{20,16},{24,20},{28,24},{32,28},... | collective-permute-start | bytes 786440 | tf_op jit(solution)/shard_map/ppermute | solution.py:132
  32.1 8.2 %collective-permute-done = bf16[4,128,256]{2,1,0:T(8,128)(2,1)S(1)} collective-permute-done((bf16[4,128,256]{2,1,0:T(8,128)(2,1)S(1)}, bf16[4,128,256]{2,1,0:T(8,128)(2,1)S(1)}, u32[]{:S(2)}, u32[]{:S(2)}) %collective-permute-start) | collective-permute-done | bytes 262176 | tf_op jit(solution)/shard_map/ppermute | solution.py:142
  40.2 4.6 %collective-permute-done.1 = bf16[4,128,256]{2,1,0:T(8,128)(2,1)S(1)} collective-permute-done((bf16[4,128,256]{2,1,0:T(8,128)(2,1)S(1)}, bf16[4,128,256]{2,1,0:T(8,128)(2,1)S(1)}, u32[]{:S(2)}, u32[]{:S(2)}) %collective-permute-start.1) | collective-permute-done | bytes 262176 | tf_op jit(solution)/shard_map/ppermute | solution.py:132
  44.8 0.0 collective-permute-done.2
  44.8 0.0 all-to-all-done.own
  44.8 2.0 %collective-permute-start.5 = (bf16[4,128,256]{2,1,0:T(8,128)(2,1)S(1)}, bf16[4,128,256]{2,1,0:T(8,128)(2,1)S(1)}, u32[]{:S(2)}, u32[]{:S(2)}) collective-permute-start(bf16[4,128,256]{2,1,0:T(8,128)(2,1)S(1)} %all-to-all-done.own), channel_id=1, source_target_pairs={{0,8},{1,57},{2,10},{3,59},{4,12},{5,61},{6,14},{7,63},{8,16},{9,1... | collective-permute-start | bytes 786440 | tf_op jit(solution)/shard_map/ppermute | solution.py:142
  46.8 3.6 %collective-permute-start.4 = (bf16[4,128,256]{2,1,0:T(8,128)(2,1)S(1)}, bf16[4,128,256]{2,1,0:T(8,128)(2,1)S(1)}, u32[]{:S(2)}, u32[]{:S(2)}) collective-permute-start(bf16[4,128,256]{2,1,0:T(8,128)(2,1)S(1)} %all-to-all-done.own), channel_id=1, source_target_pairs={{0,4},{4,8},{8,12},{12,16},{16,20},{20,24},{24,28},{28,32},{32,36}... | collective-permute-start | bytes 786440 | tf_op jit(solution)/shard_map/ppermute | solution.py:132
  50.5 3.4 %collective-permute-start.3 = (bf16[4,128,256]{2,1,0:T(8,128)(2,1)S(1)}, bf16[4,128,256]{2,1,0:T(8,128)(2,1)S(1)}, u32[]{:S(2)}, u32[]{:S(2)}) collective-permute-start(bf16[4,128,256]{2,1,0:T(8,128)(2,1)S(1)} %all-to-all-done.own), channel_id=1, source_target_pairs={{0,60},{4,0},{8,4},{12,8},{16,12},{20,16},{24,20},{28,24},{32,28},... | collective-permute-start | bytes 786440 | tf_op jit(solution)/shard_map/ppermute | solution.py:132
  53.9 0.8 add_convert_fusion
  54.8 9.0 %all-to-all-start.1 = ((bf16[4,128,256]{2,1,0:T(8,128)(2,1)}), bf16[4,128,256]{2,1,0:T(8,128)(2,1)S(1)}, u32[]{:S(2)}, u32[]{:S(2)}) async-start(bf16[4,128,256]{2,1,0:T(8,128)(2,1)} %add_convert_fusion), calls=%async_computation.1 | async-start | bytes 524288 | tf_op jit(solution)/shard_map/all_to_all | solution.py:187
  63.8 1.2 %shard_map.78 = (bf16[8,128,128]{2,1,0:T(8,128)(2,1)S(1)}, bf16[8,128,128]{2,1,0:T(8,128)(2,1)S(1)}, bf16[2,8,128,128]{3,2,1,0:T(8,128)(2,1)S(1)}) custom-call(s32[2,32]{1,0:T(2,128)S(1)} %bitcast.23, s32[1,1]{1,0:T(1,128)S(6)} %copy.8.live_count, s32[1,1]{1,0:T(1,128)} %bitcast.1.plane, s32[1,2]{1,0:T(1,128)S(1)} %add_bitcast_fusion.dp_place, ...), custom_call_target="tpu_custom_call" | custom-call | flops 1000 | bytes 3 | tf_op jit(solution)/shard_map/pallas_call | solution.py:100
  65.1 1.9 %collective-permute-start.6 = (bf16[2,8,128,128]{3,2,1,0:T(8,128)(2,1)S(1)}, bf16[2,8,128,128]{3,2,1,0:T(8,128)(2,1)S(1)}, u32[]{:S(2)}, u32[]{:S(2)}) collective-permute-start(bf16[2,8,128,128]{3,2,1,0:T(8,128)(2,1)S(1)} %get-tuple-element.29), channel_id=1, source_target_pairs={{0,1},{1,0},{2,3},{3,2},{4,5},{5,4},{6,7},{7,6},{8,9},{9,8},{10,11... | collective-permute-start | bytes 1572872 | tf_op jit(solution)/shard_map/ppermute | solution.py:146
  67.0 1.2 %shard_map.77 = (bf16[4,128,128]{2,1,0:T(8,128)(2,1)S(1)}, bf16[4,128,128]{2,1,0:T(8,128)(2,1)S(1)}) custom-call(s32[2,32]{1,0:T(2,128)S(1)} %bitcast.24, s32[1,1]{1,0:T(1,128)S(6)} %copy.8.live_count, s32[1,1]{1,0:T(1,128)} %bitcast.1.plane, s32[1,2]{1,0:T(1,128)S(1)} %add_bitcast_fusion.dp_place, bf16[128,1024]{1,0:T(8,128)(2,1)S(1)} %copy-done.2, ...), custom_call_target="tpu_custom_call" | custom-call | flops 1000 | bytes 3 | tf_op jit(solution)/shard_map/pallas_call | solution.py:100
  68.2 0.6 collective-permute-done.6
  68.9 0.1 fusion.2
  68.9 2.7 %collective-permute-start.7 = (bf16[4,128,128]{2,1,0:T(8,128)(2,1)S(1)}, bf16[4,128,128]{2,1,0:T(8,128)(2,1)S(1)}, u32[]{:S(2)}, u32[]{:S(2)}) collective-permute-start(bf16[4,128,128]{2,1,0:T(8,128)(2,1)S(1)} %get-tuple-element.30), channel_id=1, source_target_pairs={{0,64},{64,0},{128,192},{192,128},{256,320},{320,256},{384,448},{4... | collective-permute-start | bytes 393224 | tf_op jit(solution)/shard_map/ppermute | solution.py:146
  71.6 2.8 %collective-permute-start.8 = (bf16[8,128,128]{2,1,0:T(8,128)(2,1)S(1)}, bf16[8,128,128]{2,1,0:T(8,128)(2,1)S(1)}, u32[]{:S(2)}, u32[]{:S(2)}) collective-permute-start(bf16[8,128,128]{2,1,0:T(8,128)(2,1)S(1)} %fusion.2), channel_id=1, source_target_pairs={{0,2},{1,3},{2,0},{3,1},{4,6},{5,7},{6,4},{7,5},{8,10},{9,11},{10,... | collective-permute-start | bytes 786440 | tf_op jit(solution)/shard_map/ppermute | solution.py:146
  74.5 7.0 %all-to-all-done.1.parts = bf16[4,128,256]{2,1,0:T(8,128)(2,1)S(1)} async-done(((bf16[4,128,256]{2,1,0:T(8,128)(2,1)}), bf16[4,128,256]{2,1,0:T(8,128)(2,1)S(1)}, u32[]{:S(2)}, u32[]{:S(2)}) %all-to-all-start.1) | async-done | bytes 262176 | tf_op jit(solution)/shard_map/all_to_all | solution.py:187
  81.5 0.7 shard_map.79
  82.1 0.7 add_convert_fusion.1
  82.8 4.3 %all-to-all-start.2 = ((bf16[4,128,128]{2,1,0:T(8,128)(2,1)}), bf16[4,128,128]{2,1,0:T(8,128)(2,1)S(1)}, u32[]{:S(2)}, u32[]{:S(2)}) async-start(bf16[4,128,128]{2,1,0:T(8,128)(2,1)} %add_convert_fusion.1), calls=%async_computation.2 | async-start | bytes 262144 | tf_op jit(solution)/shard_map/all_to_all | solution.py:215
  87.1 0.8 fusion.1
  88.0 5.2 %all-to-all-done.2 = bf16[4,128,128]{2,1,0:T(8,128)(2,1)S(1)} async-done(((bf16[4,128,128]{2,1,0:T(8,128)(2,1)}), bf16[4,128,128]{2,1,0:T(8,128)(2,1)S(1)}, u32[]{:S(2)}, u32[]{:S(2)}) %all-to-all-start.2) | async-done | bytes 131104 | tf_op jit(solution)/shard_map/all_to_all | solution.py:215
  93.1 0.6 fusion.3
  (15 shorter events, 0.0 us)
Async XLA Ops:
  2.2 15.9 %copy-start.2 = (bf16[128,1024]{1,0:T(8,128)(2,1)S(1)}, bf16[128,1024]{1,0:T(8,128)(2,1)}, u32[]{:S(2)}) copy-start(bf16[128,1024]{1,0:T(8,128)(2,1)} %tokens.5) | copy-start | bytes 786436
  2.2 42.6 %all-to-all-start = ((bf16[4,128,256]{2,1,0:T(8,128)(2,1)}), bf16[4,128,256]{2,1,0:T(8,128)(2,1)S(1)}, u32[]{:S(2)}, u32[]{:S(2)}) async-start(bf16[4,128,256]{2,1,0:T(8,128)(2,1)} %broadcast_in_dim.13), calls=%async_computation | async-start | bytes 524288 | tf_op jit(solution)/shard_map/all_to_all | solution.py:172
  18.1 0.7 copy-start.3
  18.8 1.2 %copy-start = (bf16[1,1,32,128,128]{4,3,2,1,0:T(8,128)(2,1)S(1)}, bf16[1,1,32,128,128]{4,3,2,1,0:T(8,128)(2,1)}, u32[]{:S(2)}) copy-start(bf16[1,1,32,128,128]{4,3,2,1,0:T(8,128)(2,1)} %param.6) | copy-start | bytes 3145732
  21.6 18.6 %collective-permute-start = (bf16[4,128,256]{2,1,0:T(8,128)(2,1)S(1)}, bf16[4,128,256]{2,1,0:T(8,128)(2,1)S(1)}, u32[]{:S(2)}, u32[]{:S(2)}) collective-permute-start(bf16[4,128,256]{2,1,0:T(8,128)(2,1)S(1)} %get-tuple-element.22), channel_id=1, source_target_pairs={{0,8},{1,57},{2,10},{3,59},{4,12},{5,61},{6,14},{7,63},{8,16},{9,1... | collective-permute-start | bytes 786440 | tf_op jit(solution)/shard_map/ppermute | solution.py:142
  25.0 19.8 %collective-permute-start.1 = (bf16[4,128,256]{2,1,0:T(8,128)(2,1)S(1)}, bf16[4,128,256]{2,1,0:T(8,128)(2,1)S(1)}, u32[]{:S(2)}, u32[]{:S(2)}) collective-permute-start(bf16[4,128,256]{2,1,0:T(8,128)(2,1)S(1)} %get-tuple-element.23), channel_id=1, source_target_pairs={{0,4},{4,8},{8,12},{12,16},{16,20},{20,24},{24,28},{28,32},{32,36}... | collective-permute-start | bytes 786440 | tf_op jit(solution)/shard_map/ppermute | solution.py:132
  28.0 16.9 %collective-permute-start.2 = (bf16[4,128,256]{2,1,0:T(8,128)(2,1)S(1)}, bf16[4,128,256]{2,1,0:T(8,128)(2,1)S(1)}, u32[]{:S(2)}, u32[]{:S(2)}) collective-permute-start(bf16[4,128,256]{2,1,0:T(8,128)(2,1)S(1)} %get-tuple-element.24), channel_id=1, source_target_pairs={{0,60},{4,0},{8,4},{12,8},{16,12},{20,16},{24,20},{28,24},{32,28},... | collective-permute-start | bytes 786440 | tf_op jit(solution)/shard_map/ppermute | solution.py:132
  44.8 19.0 %collective-permute-start.5 = (bf16[4,128,256]{2,1,0:T(8,128)(2,1)S(1)}, bf16[4,128,256]{2,1,0:T(8,128)(2,1)S(1)}, u32[]{:S(2)}, u32[]{:S(2)}) collective-permute-start(bf16[4,128,256]{2,1,0:T(8,128)(2,1)S(1)} %all-to-all-done.own), channel_id=1, source_target_pairs={{0,8},{1,57},{2,10},{3,59},{4,12},{5,61},{6,14},{7,63},{8,16},{9,1... | collective-permute-start | bytes 786440 | tf_op jit(solution)/shard_map/ppermute | solution.py:142
  46.8 16.9 %collective-permute-start.4 = (bf16[4,128,256]{2,1,0:T(8,128)(2,1)S(1)}, bf16[4,128,256]{2,1,0:T(8,128)(2,1)S(1)}, u32[]{:S(2)}, u32[]{:S(2)}) collective-permute-start(bf16[4,128,256]{2,1,0:T(8,128)(2,1)S(1)} %all-to-all-done.own), channel_id=1, source_target_pairs={{0,4},{4,8},{8,12},{12,16},{16,20},{20,24},{24,28},{28,32},{32,36}... | collective-permute-start | bytes 786440 | tf_op jit(solution)/shard_map/ppermute | solution.py:132
  50.5 13.3 %collective-permute-start.3 = (bf16[4,128,256]{2,1,0:T(8,128)(2,1)S(1)}, bf16[4,128,256]{2,1,0:T(8,128)(2,1)S(1)}, u32[]{:S(2)}, u32[]{:S(2)}) collective-permute-start(bf16[4,128,256]{2,1,0:T(8,128)(2,1)S(1)} %all-to-all-done.own), channel_id=1, source_target_pairs={{0,60},{4,0},{8,4},{12,8},{16,12},{20,16},{24,20},{28,24},{32,28},... | collective-permute-start | bytes 786440 | tf_op jit(solution)/shard_map/ppermute | solution.py:132
  54.8 12.2 %copy-start.1 = (bf16[1,1,32,128,128]{4,3,2,1,0:T(8,128)(2,1)S(1)}, bf16[1,1,32,128,128]{4,3,2,1,0:T(8,128)(2,1)}, u32[]{:S(2)}) copy-start(bf16[1,1,32,128,128]{4,3,2,1,0:T(8,128)(2,1)} %param.6) | copy-start | bytes 3145732
  54.8 26.7 %all-to-all-start.1 = ((bf16[4,128,256]{2,1,0:T(8,128)(2,1)}), bf16[4,128,256]{2,1,0:T(8,128)(2,1)S(1)}, u32[]{:S(2)}, u32[]{:S(2)}) async-start(bf16[4,128,256]{2,1,0:T(8,128)(2,1)} %add_convert_fusion), calls=%async_computation.1 | async-start | bytes 524288 | tf_op jit(solution)/shard_map/all_to_all | solution.py:187
  65.1 3.8 %collective-permute-start.6 = (bf16[2,8,128,128]{3,2,1,0:T(8,128)(2,1)S(1)}, bf16[2,8,128,128]{3,2,1,0:T(8,128)(2,1)S(1)}, u32[]{:S(2)}, u32[]{:S(2)}) collective-permute-start(bf16[2,8,128,128]{3,2,1,0:T(8,128)(2,1)S(1)} %get-tuple-element.29), channel_id=1, source_target_pairs={{0,1},{1,0},{2,3},{3,2},{4,5},{5,4},{6,7},{7,6},{8,9},{9,8},{10,11... | collective-permute-start | bytes 1572872 | tf_op jit(solution)/shard_map/ppermute | solution.py:146
  68.9 2.7 %copy-start.4 = (bf16[2,8,128,128]{3,2,1,0:T(8,128)(2,1)}, bf16[2,8,128,128]{3,2,1,0:T(8,128)(2,1)S(1)}, u32[]{:S(2)}) copy-start(bf16[2,8,128,128]{3,2,1,0:T(8,128)(2,1)S(1)} %collective-permute-done.6) | copy-start | bytes 1572868
  68.9 13.2 %collective-permute-start.7 = (bf16[4,128,128]{2,1,0:T(8,128)(2,1)S(1)}, bf16[4,128,128]{2,1,0:T(8,128)(2,1)S(1)}, u32[]{:S(2)}, u32[]{:S(2)}) collective-permute-start(bf16[4,128,128]{2,1,0:T(8,128)(2,1)S(1)} %get-tuple-element.30), channel_id=1, source_target_pairs={{0,64},{64,0},{128,192},{192,128},{256,320},{320,256},{384,448},{4... | collective-permute-start | bytes 393224 | tf_op jit(solution)/shard_map/ppermute | solution.py:146
  71.6 15.5 %collective-permute-start.8 = (bf16[8,128,128]{2,1,0:T(8,128)(2,1)S(1)}, bf16[8,128,128]{2,1,0:T(8,128)(2,1)S(1)}, u32[]{:S(2)}, u32[]{:S(2)}) collective-permute-start(bf16[8,128,128]{2,1,0:T(8,128)(2,1)S(1)} %fusion.2), channel_id=1, source_target_pairs={{0,2},{1,3},{2,0},{3,1},{4,6},{5,7},{6,4},{7,5},{8,10},{9,11},{10,... | collective-permute-start | bytes 786440 | tf_op jit(solution)/shard_map/ppermute | solution.py:146
  82.1 5.0 %copy-start.5 = (bf16[2,8,128,128]{3,2,1,0:T(8,128)(2,1)S(1)}, bf16[2,8,128,128]{3,2,1,0:T(8,128)(2,1)}, u32[]{:S(2)}) copy-start(bf16[2,8,128,128]{3,2,1,0:T(8,128)(2,1)} %copy-done.4) | copy-start | bytes 1572868
  82.8 10.3 %all-to-all-start.2 = ((bf16[4,128,128]{2,1,0:T(8,128)(2,1)}), bf16[4,128,128]{2,1,0:T(8,128)(2,1)S(1)}, u32[]{:S(2)}, u32[]{:S(2)}) async-start(bf16[4,128,128]{2,1,0:T(8,128)(2,1)} %add_convert_fusion.1), calls=%async_computation.2 | async-start | bytes 262144 | tf_op jit(solution)/shard_map/all_to_all | solution.py:215
